TPU v7x, 512 devices: a whole 4x4x16 slice. The times are simulated.
512 devices in a mesh: gz: 32 (over z_lo, y), xy: 16 (over z_hi, x, core).
Axes of the slice: x: 4, y: 4, z: 16 (z_hi: 2, z_lo: 8; z = z_hi * 8 + z_lo), core: 2. Of those that a mesh axis runs over, the one named last changes fastest.
Arguments:
- up_source: bfloat16 [32, 2, 32, 4096], P('gz', None, None, 'xy'), may hold values from -6 to 6
- down_source: bfloat16 [32, 2, 32, 4096], P('gz', None, None, 'xy'), may hold values from -6 to 6
- source_layer: int32 [32], replicated, may hold values from 0 to 31, as said below
- u_factor: bfloat16 [32, 16, 16, 2, 128, 256], P('gz', 'xy'), may hold values from -0.078125 to 0.078125
- v_factor: bfloat16 [32, 16, 16, 2, 128, 256], P('gz', 'xy'), may hold values from -0.25 to 0.25
- block_rank: int32 [32, 16, 16], P('gz', 'xy'), may hold values from 1 to 4
Outputs:
- up_trace: bfloat16 [32, 2, 32, 4096], P('gz', None, None, 'xy')
- down_trace: bfloat16 [32, 2, 32, 4096], P('gz', None, None, 'xy')
Inputs may be any that keep to these rules, and one draw needn't show every extreme that they name: `source_layer`: the index of the layer slab in which source s lies; source 0 lies in slab 0 and source 1 in slab 32 - 1. `block_rank`: block (i, j) of interface l has rank 32 times this number.
All inputs are finite; a program needn't handle non-finite values.
Results may differ from a plain program's by a relative error of at most 0.007.
Values may be sent and summed in bfloat16 or wider, within the bound.
No kernel may reach another device: no remote copies, remote signals or barrier semaphores. Data moves between devices by JAX's collectives and lax.ppermute only.
A program may use at most 64 MiB of HBM per device.

v0:
```python
import jax
import jax.numpy as jnp
from jax import lax
from jax.sharding import PartitionSpec as P

STEPS = 3


def from_behind(block, axis, distance):
    devices = range(lax.axis_size(axis))
    route = [(i - distance, i) for i in devices if i - distance in devices]
    return lax.ppermute(block, axis, route)


def complex_parts(product):
    real = product[..., 0, :, 0, :] - product[..., 1, :, 1, :]
    imag = product[..., 0, :, 1, :] + product[..., 1, :, 0, :]
    return jnp.stack([real, imag], axis=-3)


def advance(up_part, down_part, active_up, active_down, u_layer, v_layer, keep_rank):
    sources = up_part.shape[1]
    own_rows = u_layer.shape[0]
    blocks = u_layer.shape[1]
    width = u_layer.shape[-1]
    gathered = lax.all_gather(up_part, "xy", axis=2, tiled=True)
    pieces = gathered.reshape(2, sources, blocks, width)
    up_coef = complex_parts(
        jnp.einsum("asjb,ijcrb->ijascr", pieces, v_layer, preferred_element_type=jnp.float32)
    )
    up_coef = jnp.where(keep_rank[:, :, None, None, :], up_coef, 0.0).astype(jnp.bfloat16)
    forward = complex_parts(
        jnp.einsum("ijasr,ijcrb->iascb", up_coef, u_layer, preferred_element_type=jnp.float32)
    )
    forward = jnp.transpose(forward, (1, 2, 0, 3)).reshape(2, sources, own_rows * width)
    arrived = from_behind(forward, "gz", 1)
    new_up = (active_up.astype(jnp.float32) + arrived).astype(jnp.bfloat16)
    upper = from_behind(down_part, "gz", -1)
    upper_blocks = upper.reshape(2, sources, own_rows, width)
    down_coef = complex_parts(
        jnp.einsum("asib,ijcrb->ijascr", upper_blocks, u_layer, preferred_element_type=jnp.float32)
    )
    down_coef = jnp.where(keep_rank[:, :, None, None, :], down_coef, 0.0).astype(jnp.bfloat16)
    summed = lax.psum_scatter(
        complex_parts(
            jnp.einsum("ijasr,ijcrb->jascb", down_coef, v_layer, preferred_element_type=jnp.float32)
        ),
        "xy",
        scatter_dimension=0,
        tiled=True,
    )
    backward = jnp.transpose(summed, (1, 2, 0, 3)).reshape(2, sources, own_rows * width)
    new_down = (active_down.astype(jnp.float32) + backward).astype(jnp.bfloat16)
    return (new_up, new_down)


def on_device(up_source, down_source, source_layer, u_factor, v_factor, block_rank):
    layer_index = lax.axis_index("gz")
    up_mask = (layer_index >= source_layer)[None, :, None]
    down_mask = (layer_index <= source_layer)[None, :, None]
    active_up = jnp.where(up_mask, up_source[0], jnp.zeros_like(up_source[0]))
    active_down = jnp.where(down_mask, down_source[0], jnp.zeros_like(down_source[0]))
    u_layer = u_factor[0]
    v_layer = v_factor[0]
    rank_units = block_rank[0]
    max_rank = u_layer.shape[-2]
    keep_rank = (
        jnp.arange(max_rank, dtype=jnp.int32)[None, None, :]
        < max_rank // 4 * rank_units[:, :, None]
    )
    up_trace = active_up
    down_trace = active_down
    for sweep_index in range(STEPS):
        up_trace, down_trace = advance(
            up_trace, down_trace, active_up, active_down, u_layer, v_layer, keep_rank
        )
    return (up_trace[None], down_trace[None])


def solution(mesh):
    in_specs = (
        P("gz", None, None, "xy"),
        P("gz", None, None, "xy"),
        P(),
        P("gz", "xy", None, None, None, None),
        P("gz", "xy", None, None, None, None),
        P("gz", "xy", None),
    )
    out_specs = (P("gz", None, None, "xy"), P("gz", None, None, "xy"))
    return jax.shard_map(
        on_device, mesh=mesh, in_specs=in_specs, out_specs=out_specs, check_vma=False
    )
```

profile of v0, /device:TPU:1, one launch (start us, length us, event | category | flops | bytes accessed | tf_op | source)
XLA Modules:
  0.0 552.9 jit_solution(1346460437685965742)
XLA Ops:
  7.2 0.0 reduce-scatter.6.cloned.1.call-start
  7.2 0.8 broadcast_compare_fusion
  8.0 0.8 bitcast_select_fusion
  8.9 1.3 collective-permute-start.3
  10.2 0.7 multiply_bitcast_fusion
  10.8 0.8 bitcast_select_fusion.2
  11.6 54.7 %all_gather.9 = bf16[2,32,4096]{2,1,0:T(8,128)(2,1)S(1)} all-gather(bf16[2,32,256]{2,1,0:T(8,128)(2,1)S(1)} %bitcast_select_fusion.2), channel_id=1, replica_groups=mesh['gz'=32,'xy'=16] {'xy'}, dimensions={2}, use_global_device_ids=true | all-gather | bytes 557056 | tf_op jit(solution)/shard_map/all_gather | solution.py:26
  66.4 0.1 copy.128
  66.6 0.7 fusion.32
  67.4 0.1 iota_compare_fusion
  67.4 0.7 copy-done.1
  68.1 0.7 fusion.35
  68.9 0.1 fusion.91
  69.0 0.4 fusion.22
  69.4 0.1 fusion.65
  69.6 1.1 pad_maximum_fusion
  70.7 0.0 reduce-scatter.6.cloned.1.call-update
  70.7 0.0 reduce-scatter.8.cloned.1.call-start
  70.8 2.1 fusion.44
  72.9 1.7 collective-permute-start
  74.6 1.3 collective-permute-done
  75.9 0.1 fusion.112
  76.0 36.7 %all_gather.10 = bf16[2,32,4096]{2,1,0:T(8,128)(2,1)S(1)} all-gather(bf16[2,32,256]{2,1,0:T(8,128)(2,1)S(1)} %fusion.112), channel_id=1, replica_groups=mesh['gz'=32,'xy'=16] {'xy'}, dimensions={2}, use_global_device_ids=true | all-gather | bytes 557056 | tf_op jit(solution)/shard_map/all_gather | solution.py:26
  112.7 0.1 copy.129
  112.8 0.8 bitcast_bitcast_fusion.1
  113.7 55.5 %reduce-scatter.6.cloned.1.call-done = f32[1,2,32,256]{3,2,1,0:T(8,128)} async-done(((f32[16,2,32,256]{3,2,1,0:T(8,128)}), f32[1,2,32,256]{3,2,1,0:T(8,128)}) %reduce-scatter.6.cloned.1.call-update) | async-done | bytes 65552 | tf_op jit(solution)/shard_map/reduce_scatter | solution.py:44
  169.2 1.1 fusion.110
  170.3 1.3 collective-permute-start.4
  171.6 1.8 fusion.26
  173.4 1.6 collective-permute-done.4
  174.9 0.7 fusion.38
  175.7 0.1 fusion.89
  175.8 0.4 fusion.20
  176.2 0.1 fusion.63
  176.4 1.1 pad_maximum_fusion.1
  177.5 0.0 reduce-scatter.8.cloned.1.call-update
  177.5 0.0 all-reduce.3.cloned.1.call-start
  177.5 0.1 fusion.95
  177.6 2.1 fusion.47
  179.7 3.1 collective-permute-start.1
  182.8 1.3 collective-permute-done.1
  184.1 0.1 fusion.113
  184.2 40.9 %all_gather.11 = bf16[2,32,4096]{2,1,0:T(8,128)(2,1)S(1)} all-gather(bf16[2,32,256]{2,1,0:T(8,128)(2,1)S(1)} %fusion.113), channel_id=1, replica_groups=mesh['gz'=32,'xy'=16] {'xy'}, dimensions={2}, use_global_device_ids=true | all-gather | bytes 557056 | tf_op jit(solution)/shard_map/all_gather | solution.py:26
  225.1 0.1 copy.130
  225.2 0.8 bitcast_bitcast_fusion
  226.1 54.3 %reduce-scatter.8.cloned.1.call-done = f32[1,2,32,256]{3,2,1,0:T(8,128)} async-done(((f32[16,2,32,256]{3,2,1,0:T(8,128)}), f32[1,2,32,256]{3,2,1,0:T(8,128)}) %reduce-scatter.8.cloned.1.call-update) | async-done | bytes 65552 | tf_op jit(solution)/shard_map/reduce_scatter | solution.py:44
  280.4 1.1 fusion.111
  281.5 1.3 collective-permute-start.5
  282.8 1.8 fusion.29
  284.6 1.6 collective-permute-done.5
  286.1 0.7 fusion.41
  286.9 0.1 fusion.87
  287.0 0.4 fusion
  287.4 0.1 fusion.59
  287.5 0.1 fusion.61
  287.6 1.1 pad_maximum_fusion.2
  288.7 0.0 all-reduce.3.cloned.1.call-update
  288.7 0.1 fusion.93
  288.8 2.1 fusion.50
  290.9 3.1 collective-permute-start.2
  294.1 1.3 dynamic-slice
  295.4 0.7 fusion.117
  296.1 248.1 %all-reduce.3.cloned.1.call-done = f32[16,2,32,256]{3,2,0,1:T(8,128)} async-done(((f32[16,2,32,256]{3,2,0,1:T(8,128)}), f32[16,2,32,256]{3,2,0,1:T(8,128)}) %all-reduce.3.cloned.1.call-update) | async-done | bytes 1048592
  544.2 2.2 fusion.116
  (22 shorter events, 0.2 us)
Async XLA Ops:
  7.2 59.4 %copy-start = (bf16[1,1,16,2,128,256]{5,4,3,2,1,0:T(8,128)(2,1)S(1)}, bf16[1,1,16,2,128,256]{5,4,3,2,1,0:T(8,128)(2,1)}, u32[]{:S(2)}) copy-start(bf16[1,1,16,2,128,256]{5,4,3,2,1,0:T(8,128)(2,1)} %param.10) | copy-start | bytes 6291460
  7.2 162.0 %reduce-scatter.6.cloned.1.call-start = ((), (), s32[]{:S(2)}) async-start(), calls=%async_computation.2 | async-start | bytes 1114112 | tf_op jit(solution)/shard_map/reduce_scatter | solution.py:44
  8.9 58.6 %collective-permute-start.3 = (bf16[2,32,256]{2,1,0:T(8,128)(2,1)S(1)}, bf16[2,32,256]{2,1,0:T(8,128)(2,1)S(1)}, u32[]{:S(2)}, u32[]{:S(2)}) collective-permute-start(bf16[2,32,256]{2,1,0:T(8,128)(2,1)S(1)} %bitcast_select_fusion), channel_id=1, source_target_pairs={{16,0},{32,16},{48,32},{64,48},{80,64},{96,80},{112,96},{128,112},... | collective-permute-start | bytes 98312 | tf_op jit(solution)/shard_map/ppermute | solution.py:12
  66.5 1.6 copy-start.1
  70.7 5.2 copy-start.4
  70.7 209.7 %reduce-scatter.8.cloned.1.call-start = ((), (), s32[]{:S(2)}) async-start(), calls=%async_computation.3 | async-start | bytes 1114112 | tf_op jit(solution)/shard_map/reduce_scatter | solution.py:44
  72.9 96.3 %copy-start.5 = (bf16[1,2,32,256]{3,2,1,0:T(8,128)(2,1)S(1)}, bf16[1,2,32,256]{3,2,1,0:T(8,128)(2,1)}, u32[]{:S(2)}) copy-start(bf16[1,2,32,256]{3,2,1,0:T(8,128)(2,1)} %param.7) | copy-start | bytes 98308
  72.9 3.0 collective-permute-start
  169.2 5.7 %copy-start.2 = (bf16[1,1,16,2,128,256]{5,4,3,2,1,0:T(8,128)(2,1)S(1)}, bf16[1,1,16,2,128,256]{5,4,3,2,1,0:T(8,128)(2,1)}, u32[]{:S(2)}) copy-start(bf16[1,1,16,2,128,256]{5,4,3,2,1,0:T(8,128)(2,1)} %param.9) | copy-start | bytes 6291460
  170.3 4.6 collective-permute-start.4
  177.5 366.7 %all-reduce.3.cloned.1.call-start = ((), (), s32[]{:S(2)}) async-start(), calls=%async_computation.4 | async-start | bytes 2097152
  179.7 4.4 collective-permute-start.1
  280.4 5.7 %copy-start.3 = (bf16[1,1,16,2,128,256]{5,4,3,2,1,0:T(8,128)(2,1)S(1)}, bf16[1,1,16,2,128,256]{5,4,3,2,1,0:T(8,128)(2,1)}, u32[]{:S(2)}) copy-start(bf16[1,1,16,2,128,256]{5,4,3,2,1,0:T(8,128)(2,1)} %param.9) | copy-start | bytes 6291460
  281.5 4.6 collective-permute-start.5
  290.9 4.5 collective-permute-start.2
Sparse Core Ops, SparseCore 0:
  70.8 98.3 reduce-scatter.5
  177.6 102.7 reduce-scatter.7
  288.8 255.3 all-reduce.2
where the time goes:
time: 554 us; the launch traced here: 553 us
  waiting for transfers between devices  364 us (66%)
  blocking collectives  132 us (24%)
  matrix products  14.1 us (3%)
  between operations  14 us (3%)
  other arithmetic  12.6 us (2%)
  starting transfers between devices  11.9 us (2%)
    unnamed x4, waiting for transfers between devices  248 us
    all_gather x3, blocking collectives, advance(): gathered = lax.all_gather(up_part, 'xy', axis=2, tiled=True)  132 us
    reduce_scatter x2, waiting for transfers between devices, advance(): lax.psum_scatter(complex_parts(jnp.einsum('ijasr,ijcrb->jascb', down_coef...  110 us
    ppermute x6, starting transfers between devices, from_behind(): return lax.ppermute(block, axis, route)  11.8 us
  transfers between devices with their start and end apart: 9, of which 7 were waited for; matrix products, arithmetic and copies ran while one was open for 3% of the time, Pallas kernels for 0%

commit v1 on v0

v1 whole, which is shorter than its diff:
```python
import functools

import jax
import jax.numpy as jnp
from jax import lax
from jax.experimental import pallas as pl
from jax.experimental.pallas import tpu as pltpu
from jax.sharding import PartitionSpec as P

STEPS = 3
XS = 4
PAIR = 2
ROWS = 64
HALF = 32
BF = jnp.bfloat16
F32 = jnp.float32


def dot_rows(a, b):
    return lax.dot_general(a, b, (((1,), (1,)), ((), ())), preferred_element_type=F32)


def dot_cols(a, b):
    return lax.dot_general(a, b, (((1,), (0,)), ((), ())), preferred_element_type=F32)


def coefficients(product, limit):
    rank = product.shape[1] // 2
    real = product[:HALF, :rank] - product[HALF:, rank:]
    imag = product[:HALF, rank:] + product[HALF:, :rank]
    keep = lax.broadcasted_iota(jnp.int32, real.shape, 1) < limit
    real = jnp.where(keep, real, 0.0).astype(BF)
    imag = jnp.where(keep, imag, 0.0).astype(BF)
    top = jnp.concatenate([real, -imag], axis=1)
    bottom = jnp.concatenate([imag, real], axis=1)
    return jnp.concatenate([top, bottom], axis=0)


def block_of(x, z, c):
    return z * 8 + x * 2 + c


def spread_kernel(where_ref, rank_ref, hop_ref, far_ref, own0_ref, far0_ref, next_ref, u0_ref, v0_ref, u1_ref, v1_ref, out_ref):
    core = where_ref[0]
    z_own = where_ref[1]
    first_layer = where_ref[2] == 0

    @pl.when(core == 0)
    def _():
        for c in range(PAIR):
            own = jnp.where(first_layer, own0_ref[c], hop_ref[c])
            far = jnp.where(first_layer, far0_ref[c], far_ref[c])
            for z in range(2):
                block = jnp.where(z_own == z, own, far)
                for x in range(XS):
                    out_ref[x, z * PAIR + c] = block

    @pl.when(core == 1)
    def _():
        traces = []
        for c in range(PAIR):
            total = next_ref[c].astype(F32) + (hop_ref[c].astype(F32) + far_ref[c].astype(F32))
            traces.append(total.astype(BF))
        factors = ((1, u0_ref, v0_ref), (0, u1_ref, v1_ref))
        for x in range(XS):
            for z in range(2):
                for c in range(PAIR):
                    j = block_of(x, z, c)
                    total = None
                    for row, u_ref, v_ref in factors:
                        product = dot_rows(traces[row], u_ref[j])
                        coef = coefficients(product, rank_ref[row, j])
                        part = dot_cols(coef, v_ref[j])
                        total = part if total is None else total + part
                    out_ref[x, z * PAIR + c] = total.astype(BF)


def gather_kernel(where_ref, rank_ref, got_ref, next_ref, u0_ref, v0_ref, u1_ref, v1_ref, hop_ref, far_ref):
    core = where_ref[0]
    z_own = where_ref[1]

    @pl.when(core == 0)
    def _():
        factors = ((0, u0_ref, v0_ref), (1, u1_ref, v1_ref))
        for row, u_ref, v_ref in factors:
            total = next_ref[row].astype(F32)
            for x in range(XS):
                for z in range(2):
                    for c in range(PAIR):
                        j = block_of(x, z, c)
                        product = dot_rows(got_ref[x, z * PAIR + c], v_ref[j])
                        coef = coefficients(product, rank_ref[row, j])
                        total = total + dot_cols(coef, u_ref[j])
            block = total.astype(BF)
            hop_ref[row] = block
            far_ref[row] = block

    @pl.when(core == 1)
    def _():
        for c in range(PAIR):
            sums = []
            for z in range(2):
                total = got_ref[0, z * PAIR + c].astype(F32)
                for x in range(1, XS):
                    total = total + got_ref[x, z * PAIR + c].astype(F32)
                sums.append(total.astype(BF))
            hop_ref[c] = jnp.where(z_own == 0, sums[0], sums[1])
            far_ref[c] = jnp.where(z_own == 0, sums[1], sums[0])


def call(kernel, outs, scalars, arrays):
    smem = pl.BlockSpec(memory_space=pltpu.SMEM)
    vmem = pl.BlockSpec(memory_space=pltpu.VMEM)
    return pl.pallas_call(
        kernel,
        out_shape=outs,
        in_specs=[smem] * len(scalars) + [vmem] * len(arrays),
        out_specs=jax.tree.map(lambda _: vmem, outs),
        compiler_params=pltpu.CompilerParams(vmem_limit_bytes=48 * 1024 * 1024),
        cost_estimate=pl.CostEstimate(flops=64 * 2 * 64 * 256 * 256, bytes_accessed=10 * 1024 * 1024, transcendentals=0),
    )(*scalars, *arrays)


def on_device(layers, up_source, down_source, source_layer, u_factor, v_factor, block_rank):
    layer = lax.axis_index("gz")
    place = lax.axis_index("xy")
    core = place % 2
    z_own = place // 8
    both = ("gz", "xy")
    width = u_factor.shape[-1]
    max_rank = u_factor.shape[-2]
    step = max_rank // 4

    def send(block, target):
        route = []
        for l in range(layers):
            for i in range(16):
                to = target(l, i)
                if to is not None and 0 <= to[0] < layers:
                    route.append((l * 16 + i, to[0] * 16 + to[1]))
        return lax.ppermute(block, both, route)

    def ahead(l, i):
        return (l + 1, i) if i % 2 == 0 else (l - 1, i)

    def ahead_far(l, i):
        return (l + 1, i ^ 8) if i % 2 == 0 else (l - 1, i ^ 8)

    pairs = [[2 * k, 2 * k + 1] for k in range(8)]
    rings = [[block_of(x, z, c) for x in range(XS)] for z in range(2) for c in range(2)]

    up_mask = (layer >= source_layer)[None, :, None]
    down_mask = (layer <= source_layer)[None, :, None]
    active_up = jnp.where(up_mask, up_source[0], jnp.zeros_like(up_source[0])).reshape(ROWS, width)
    active_down = jnp.where(down_mask, down_source[0], jnp.zeros_like(down_source[0])).reshape(ROWS, width)
    ranks = block_rank[0, 0].astype(BF)
    rank_rows = jnp.broadcast_to(jnp.pad(ranks, (0, width - ranks.shape[0]))[None, :], (16, width))
    packed = jnp.concatenate([active_up, active_down, rank_rows], axis=0)
    chip = lax.all_gather(packed, "xy", axis=0, axis_index_groups=pairs)
    mine = jnp.where(core == 0, chip[:, :ROWS], chip[:, ROWS : 2 * ROWS])
    limits = (chip[:, 2 * ROWS, :16].astype(F32) * step).astype(jnp.int32)

    u_own = u_factor[0, 0].reshape(16, 2 * max_rank, width)
    v_own = v_factor[0, 0].reshape(16, 2 * max_rank, width)
    far0 = send(mine, lambda l, i: (l, i ^ 8) if i % 2 == 0 else None)
    following = send(mine, lambda l, i: (l - 1, i))
    u_other = lax.ppermute(u_own, "xy", [(i, i ^ 1) for i in range(16)])
    v_other = lax.ppermute(v_own, "xy", [(i, i ^ 1) for i in range(16)])

    where = jnp.stack([core, z_own, layer]).astype(jnp.int32)
    scalars = (where, limits)
    factors = (u_own, v_own, u_other, v_other)
    pair_shape = jax.ShapeDtypeStruct((PAIR, ROWS, width), BF)
    ring_shape = jax.ShapeDtypeStruct((XS, 2 * PAIR, ROWS, width), BF)

    hop = jnp.where(core == 0, mine, jnp.zeros_like(mine))
    far = far0
    for sweep in range(STEPS):
        sent = call(spread_kernel, ring_shape, scalars, (hop, far, mine, far0, following) + factors)
        got = lax.all_to_all(sent, "xy", 0, 0, axis_index_groups=rings)
        near, away = call(gather_kernel, (pair_shape, pair_shape), scalars, (got, following) + factors)
        if sweep < STEPS - 1:
            far = send(away, ahead_far)
            hop = send(near, ahead)

    last = send(away, lambda l, i: (l + 1, i) if i % 2 == 0 else (l, i ^ 8))
    up_pair = jnp.where(layer == 0, mine, last)
    down_pair = (mine.astype(F32) + (near.astype(F32) + last.astype(F32))).astype(BF)
    final = jnp.where(core == 0, up_pair, down_pair)
    swapped = lax.all_gather(final[1 - core], "xy", axis=0, axis_index_groups=pairs)
    kept = final[core]
    other = swapped[1 - core]
    up_trace = jnp.where(core == 0, kept, other).reshape(up_source.shape)
    down_trace = jnp.where(core == 0, other, kept).reshape(up_source.shape)
    return up_trace, down_trace


def solution(mesh):
    in_specs = (
        P("gz", None, None, "xy"),
        P("gz", None, None, "xy"),
        P(),
        P("gz", "xy", None, None, None, None),
        P("gz", "xy", None, None, None, None),
        P("gz", "xy", None),
    )
    out_specs = (P("gz", None, None, "xy"), P("gz", None, None, "xy"))
    return jax.shard_map(
        functools.partial(on_device, mesh.shape["gz"]),
        mesh=mesh,
        in_specs=in_specs,
        out_specs=out_specs,
        check_vma=False,
    )
```

time: 554 us -> 146 us (0.26)
  the two profiles are of different devices: /device:TPU:1 before, /device:TPU:33 now
where the time goes in v1:
time: 146 us
  starting transfers between devices  56 us (38%)
  blocking collectives  45.6 us (31%)
  Pallas kernels  25.6 us (18%)
  waiting for transfers between devices  10.1 us (7%)
  local copies, waits for them, and re-layouts  4.71 us (3%)
  other arithmetic  2.95 us (2%)
    ppermute x7, starting transfers between devices, send(): return lax.ppermute(block, both, route)  51.5 us
    all_to_all x3, blocking collectives, on_device(): got = lax.all_to_all(sent, 'xy', 0, 0, axis_index_groups=rings)  30 us
    pallas_call x6, Pallas kernels, call(): pl.pallas_call(kernel, out_shape=outs, in_specs=[smem] * len(scalars) + [...  25.6 us
    all_gather x1, blocking collectives, on_device(): lax.all_gather(final[1 - core], 'xy', axis=0, axis_index_groups=pairs)  13.1 us
    ppermute x7, waiting for transfers between devices, send(): return lax.ppermute(block, both, route)  10.1 us
    unnamed x10, local copies, waits for them, and re-layouts  4.5 us
  transfers between devices with their start and end apart: 9, of which 4 were waited for; matrix products, arithmetic and copies ran while one was open for 2% of the time, Pallas kernels for 0%

profile of v1, /device:TPU:33, one launch (start us, length us, event | category | flops | bytes accessed | tf_op | source)
XLA Modules:
  0.0 145.8 jit_solution(15784373000349322899)
XLA Ops:
  0.6 2.6 %collective-permute-start.2 = (bf16[16,256,256]{2,1,0:T(8,128)(2,1)}, bf16[16,256,256]{2,1,0:T(8,128)(2,1)S(1)}, u32[]{:S(2)}, u32[]{:S(2)}) collective-permute-start(bf16[16,256,256]{2,1,0:T(8,128)(2,1)} %bitcast.15), channel_id=1, source_target_pairs={{0,1},{1,0},{2,3},{3,2},{4,5},{5,4},{6,7},{7,6},{8,9},{9,8},{10,11... | collective-permute-start | bytes 6291464 | tf_op jit(solution)/shard_map/ppermute | solution.py:167
  3.2 1.9 %collective-permute-start.3 = (bf16[16,256,256]{2,1,0:T(8,128)(2,1)}, bf16[16,256,256]{2,1,0:T(8,128)(2,1)}, u32[]{:S(2)}, u32[]{:S(2)}) collective-permute-start(bf16[16,256,256]{2,1,0:T(8,128)(2,1)} %bitcast.22), channel_id=1, source_target_pairs={{0,1},{1,0},{2,3},{3,2},{4,5},{5,4},{6,7},{7,6},{8,9},{9,8},{10,11... | collective-permute-start | bytes 6291464 | tf_op jit(solution)/shard_map/ppermute | solution.py:168
  5.2 0.7 broadcast_compare_fusion.1
  5.8 0.1 broadcast_in_dim.33
  5.9 0.1 broadcast_in_dim.36
  6.0 0.7 convert_bitcast_fusion
  6.7 0.9 bitcast_select_fusion
  7.6 2.5 %all-gather = bf16[288,256]{1,0:T(8,128)(2,1)S(1)} all-gather(bf16[144,256]{1,0:T(8,128)(2,1)S(1)} %pad_maximum_fusion), channel_id=2, replica_groups={{0,1},{2,3},{4,5},{6,7},{8,9},{10,11},{12,13},{14,15},{16,17},{18,19},{..., dimensions={0}, use_global_device_ids=true | all-gather | bytes 221184 | tf_op jit(solution)/shard_map/all_gather | solution.py:159
  10.1 0.7 collective-permute-start
  10.8 4.2 %collective-permute-start.1 = (bf16[2,64,256]{2,1,0:T(8,128)(2,1)S(1)}, bf16[2,64,256]{2,1,0:T(8,128)(2,1)S(1)}, u32[]{:S(2)}, u32[]{:S(2)}) collective-permute-start(bf16[2,64,256]{2,1,0:T(8,128)(2,1)S(1)} %get-tuple-element.15.own0_ref), channel_id=1, source_target_pairs={{16,0},{17,1},{18,2},{19,3},{20,4},{21,5},{22,6},{23,7},{24,8},{25... | collective-permute-start | bytes 196616 | tf_op jit(solution)/shard_map/ppermute | solution.py:141
  15.0 0.1 pad_add_fusion.where_ref
  15.1 0.0 collective-permute-done.far_ref.far0_ref
  15.1 1.2 collective-permute-done.1.next_ref
  16.3 0.0 collective-permute-done.2.u1_ref
  16.3 0.0 copy-start.4
  16.3 0.0 collective-permute-done.3.v1_ref
  16.3 1.3 copy-done.4
  17.6 0.0 copy-start
  17.6 1.6 %copy-done = bf16[1,1,16,2,128,256]{5,4,3,2,1,0:T(8,128)(2,1)S(1)} copy-done((bf16[1,1,16,2,128,256]{5,4,3,2,1,0:T(8,128)(2,1)S(1)}, bf16[1,1,16,2,128,256]{5,4,3,2,1,0:T(8,128)(2,1)}, u32[]{:S(2)}) %copy-start) | copy-done | bytes 2097176
  19.2 0.0 copy-start.2
  19.2 1.6 %copy-done.2 = bf16[1,1,16,2,128,256]{5,4,3,2,1,0:T(8,128)(2,1)S(1)} copy-done((bf16[1,1,16,2,128,256]{5,4,3,2,1,0:T(8,128)(2,1)S(1)}, bf16[1,1,16,2,128,256]{5,4,3,2,1,0:T(8,128)(2,1)}, u32[]{:S(2)}) %copy-start.2) | copy-done | bytes 2097176
  20.8 0.0 copy-start.1
  20.8 0.0 copy-start.3
  20.8 6.3 %shard_map.77 = bf16[4,4,64,256]{3,2,1,0:T(8,128)(2,1)S(1)} custom-call(s32[3]{0:T(128)S(1)} %pad_add_fusion.where_ref, s32[2,16]{1,0:T(2,128)S(1)} %bitcast.29, bf16[2,64,256]{2,1,0:T(8,128)(2,1)S(1)} %get-tuple-element.14.hop_ref, bf16[2,64,256]{2,1,0:T(8,128)(2,1)S(1)} %collective-permute-done.far_ref.far0_ref, ...), custom_call_target="tpu_custom_call" | custom-call | flops 536870912 | bytes 10485760 | tf_op jit(solution)/shard_map/pallas_call | solution.py:114
  27.1 10.7 %all_to_all.15.got_ref = bf16[4,4,64,256]{3,2,1,0:T(8,128)(2,1)S(1)} all-to-all(bf16[4,4,64,256]{3,2,1,0:T(8,128)(2,1)S(1)} %shard_map.77), channel_id=1, replica_groups={{0,2,4,6},{1,3,5,7},{8,10,12,14},{9,11,13,15},{16,18,20,22},{17,19,21,2..., dimensions={0} | all-to-all | bytes 1048576 | tf_op jit(solution)/shard_map/all_to_all | solution.py:180
  37.9 0.0 copy-done.1
  37.9 0.0 copy-done.3
  37.9 2.3 %shard_map.78 = (bf16[2,64,256]{2,1,0:T(8,128)(2,1)S(1)}, bf16[2,64,256]{2,1,0:T(8,128)(2,1)S(1)}) custom-call(s32[3]{0:T(128)S(1)} %pad_add_fusion.where_ref, s32[2,16]{1,0:T(2,128)S(1)} %bitcast.30, bf16[4,4,64,256]{3,2,1,0:T(8,128)(2,1)S(1)} %all_to_all.15.got_ref, bf16[2,64,256]{2,1,0:T(8,128)(2,1)S(1)} %collective-permute-done.1.next_ref, ...), custom_call_target="tpu_custom_call" | custom-call | flops 536870912 | bytes 10485760 | tf_op jit(solution)/shard_map/pallas_call | solution.py:114
  40.2 5.8 %collective-permute-start.4 = (bf16[2,64,256]{2,1,0:T(8,128)(2,1)S(1)}, bf16[2,64,256]{2,1,0:T(8,128)(2,1)S(1)}, u32[]{:S(2)}, u32[]{:S(2)}) collective-permute-start(bf16[2,64,256]{2,1,0:T(8,128)(2,1)S(1)} %get-tuple-element.8), channel_id=1, source_target_pairs={{0,16},{2,18},{4,20},{6,22},{8,24},{10,26},{12,28},{14,30},{16,32}... | collective-permute-start | bytes 196616 | tf_op jit(solution)/shard_map/ppermute | solution.py:141
  46.0 14.3 %collective-permute-start.5 = (bf16[2,64,256]{2,1,0:T(8,128)(2,1)S(1)}, bf16[2,64,256]{2,1,0:T(8,128)(2,1)S(1)}, u32[]{:S(2)}, u32[]{:S(2)}) collective-permute-start(bf16[2,64,256]{2,1,0:T(8,128)(2,1)S(1)} %get-tuple-element.9), channel_id=1, source_target_pairs={{0,24},{2,26},{4,28},{6,30},{8,16},{10,18},{12,20},{14,22},{16,40}... | collective-permute-start | bytes 196616 | tf_op jit(solution)/shard_map/ppermute | solution.py:141
  60.3 0.0 collective-permute-done.4.hop_ref
  60.3 1.5 %collective-permute-done.5.far_ref = bf16[2,64,256]{2,1,0:T(8,128)(2,1)S(1)} collective-permute-done((bf16[2,64,256]{2,1,0:T(8,128)(2,1)S(1)}, bf16[2,64,256]{2,1,0:T(8,128)(2,1)S(1)}, u32[]{:S(2)}, u32[]{:S(2)}) %collective-permute-start.5) | collective-permute-done | bytes 65568 | tf_op jit(solution)/shard_map/ppermute | solution.py:141
  61.8 6.2 %shard_map.79 = bf16[4,4,64,256]{3,2,1,0:T(8,128)(2,1)S(1)} custom-call(s32[3]{0:T(128)S(1)} %pad_add_fusion.where_ref, s32[2,16]{1,0:T(2,128)S(1)} %bitcast.31, bf16[2,64,256]{2,1,0:T(8,128)(2,1)S(1)} %collective-permute-done.4.hop_ref, bf16[2,64,256]{2,1,0:T(8,128)(2,1)S(1)} %collective-permute-done.5.far_ref, ...), custom_call_target="tpu_custom_call" | custom-call | flops 536870912 | bytes 10485760 | tf_op jit(solution)/shard_map/pallas_call | solution.py:114
  67.9 9.6 %all_to_all.16.got_ref = bf16[4,4,64,256]{3,2,1,0:T(8,128)(2,1)S(1)} all-to-all(bf16[4,4,64,256]{3,2,1,0:T(8,128)(2,1)S(1)} %shard_map.79), channel_id=1, replica_groups={{0,2,4,6},{1,3,5,7},{8,10,12,14},{9,11,13,15},{16,18,20,22},{17,19,21,2..., dimensions={0} | all-to-all | bytes 1048576 | tf_op jit(solution)/shard_map/all_to_all | solution.py:180
  77.6 2.3 %shard_map.80 = (bf16[2,64,256]{2,1,0:T(8,128)(2,1)S(1)}, bf16[2,64,256]{2,1,0:T(8,128)(2,1)S(1)}) custom-call(s32[3]{0:T(128)S(1)} %pad_add_fusion.where_ref, s32[2,16]{1,0:T(2,128)S(1)} %bitcast.32, bf16[4,4,64,256]{3,2,1,0:T(8,128)(2,1)S(1)} %all_to_all.16.got_ref, bf16[2,64,256]{2,1,0:T(8,128)(2,1)S(1)} %collective-permute-done.1.next_ref, ...), custom_call_target="tpu_custom_call" | custom-call | flops 536870912 | bytes 10485760 | tf_op jit(solution)/shard_map/pallas_call | solution.py:114
  79.9 5.6 %collective-permute-start.6 = (bf16[2,64,256]{2,1,0:T(8,128)(2,1)S(1)}, bf16[2,64,256]{2,1,0:T(8,128)(2,1)S(1)}, u32[]{:S(2)}, u32[]{:S(2)}) collective-permute-start(bf16[2,64,256]{2,1,0:T(8,128)(2,1)S(1)} %get-tuple-element.10), channel_id=1, source_target_pairs={{0,16},{2,18},{4,20},{6,22},{8,24},{10,26},{12,28},{14,30},{16,32}... | collective-permute-start | bytes 196616 | tf_op jit(solution)/shard_map/ppermute | solution.py:141
  85.5 10.0 %collective-permute-start.7 = (bf16[2,64,256]{2,1,0:T(8,128)(2,1)S(1)}, bf16[2,64,256]{2,1,0:T(8,128)(2,1)S(1)}, u32[]{:S(2)}, u32[]{:S(2)}) collective-permute-start(bf16[2,64,256]{2,1,0:T(8,128)(2,1)S(1)} %get-tuple-element.11), channel_id=1, source_target_pairs={{0,24},{2,26},{4,28},{6,30},{8,16},{10,18},{12,20},{14,22},{16,40}... | collective-permute-start | bytes 196616 | tf_op jit(solution)/shard_map/ppermute | solution.py:141
  95.6 0.0 collective-permute-done.6.hop_ref
  95.6 4.6 %collective-permute-done.7.far_ref = bf16[2,64,256]{2,1,0:T(8,128)(2,1)S(1)} collective-permute-done((bf16[2,64,256]{2,1,0:T(8,128)(2,1)S(1)}, bf16[2,64,256]{2,1,0:T(8,128)(2,1)S(1)}, u32[]{:S(2)}, u32[]{:S(2)}) %collective-permute-start.7) | collective-permute-done | bytes 65568 | tf_op jit(solution)/shard_map/ppermute | solution.py:141
  100.2 6.2 %shard_map.81 = bf16[4,4,64,256]{3,2,1,0:T(8,128)(2,1)S(1)} custom-call(s32[3]{0:T(128)S(1)} %pad_add_fusion.where_ref, s32[2,16]{1,0:T(2,128)S(1)} %bitcast.33, bf16[2,64,256]{2,1,0:T(8,128)(2,1)S(1)} %collective-permute-done.6.hop_ref, bf16[2,64,256]{2,1,0:T(8,128)(2,1)S(1)} %collective-permute-done.7.far_ref, ...), custom_call_target="tpu_custom_call" | custom-call | flops 536870912 | bytes 10485760 | tf_op jit(solution)/shard_map/pallas_call | solution.py:114
  106.3 9.6 %all_to_all.17.got_ref = bf16[4,4,64,256]{3,2,1,0:T(8,128)(2,1)S(1)} all-to-all(bf16[4,4,64,256]{3,2,1,0:T(8,128)(2,1)S(1)} %shard_map.81), channel_id=1, replica_groups={{0,2,4,6},{1,3,5,7},{8,10,12,14},{9,11,13,15},{16,18,20,22},{17,19,21,2..., dimensions={0} | all-to-all | bytes 1048576 | tf_op jit(solution)/shard_map/all_to_all | solution.py:180
  116.0 2.3 %shard_map.82 = (bf16[2,64,256]{2,1,0:T(8,128)(2,1)S(1)}, bf16[2,64,256]{2,1,0:T(8,128)(2,1)S(1)}) custom-call(s32[3]{0:T(128)S(1)} %pad_add_fusion.where_ref, s32[2,16]{1,0:T(2,128)S(1)} %bitcast.34, bf16[4,4,64,256]{3,2,1,0:T(8,128)(2,1)S(1)} %all_to_all.17.got_ref, bf16[2,64,256]{2,1,0:T(8,128)(2,1)S(1)} %collective-permute-done.1.next_ref, ...), custom_call_target="tpu_custom_call" | custom-call | flops 536870912 | bytes 10485760 | tf_op jit(solution)/shard_map/pallas_call | solution.py:114
  118.3 10.9 %collective-permute-start.8 = (bf16[2,64,256]{2,1,0:T(8,128)(2,1)S(1)}, bf16[2,64,256]{2,1,0:T(8,128)(2,1)S(1)}, u32[]{:S(2)}, u32[]{:S(2)}) collective-permute-start(bf16[2,64,256]{2,1,0:T(8,128)(2,1)S(1)} %get-tuple-element.12), channel_id=1, source_target_pairs={{0,16},{1,9},{2,18},{3,11},{4,20},{5,13},{6,22},{7,15},{8,24},{9,1... | collective-permute-start | bytes 196616 | tf_op jit(solution)/shard_map/ppermute | solution.py:141
  129.2 2.8 %collective-permute-done.8 = bf16[2,64,256]{2,1,0:T(8,128)(2,1)S(1)} collective-permute-done((bf16[2,64,256]{2,1,0:T(8,128)(2,1)S(1)}, bf16[2,64,256]{2,1,0:T(8,128)(2,1)S(1)}, u32[]{:S(2)}, u32[]{:S(2)}) %collective-permute-start.8) | collective-permute-done | bytes 65568 | tf_op jit(solution)/shard_map/ppermute | solution.py:141
  132.1 13.1 %all_gather.11 = bf16[2,64,256]{2,1,0:T(8,128)(2,1)S(1)} all-gather(bf16[1,64,256]{2,1,0:T(8,128)(2,1)S(1)} %constant_dynamic-slice_fusion), channel_id=1, replica_groups={{0,1},{2,3},{4,5},{6,7},{8,9},{10,11},{12,13},{14,15},{16,17},{18,19},{..., dimensions={0}, use_global_device_ids=true | all-gather | bytes 98304 | tf_op jit(solution)/shard_map/all_gather | solution.py:190
  145.1 0.6 broadcast_select_fusion.1
  (9 shorter events, 0.1 us)
Async XLA Ops:
  0.6 15.7 %collective-permute-start.2 = (bf16[16,256,256]{2,1,0:T(8,128)(2,1)}, bf16[16,256,256]{2,1,0:T(8,128)(2,1)S(1)}, u32[]{:S(2)}, u32[]{:S(2)}) collective-permute-start(bf16[16,256,256]{2,1,0:T(8,128)(2,1)} %bitcast.15), channel_id=1, source_target_pairs={{0,1},{1,0},{2,3},{3,2},{4,5},{5,4},{6,7},{7,6},{8,9},{9,8},{10,11... | collective-permute-start | bytes 6291464 | tf_op jit(solution)/shard_map/ppermute | solution.py:167
  3.2 13.1 %collective-permute-start.3 = (bf16[16,256,256]{2,1,0:T(8,128)(2,1)}, bf16[16,256,256]{2,1,0:T(8,128)(2,1)}, u32[]{:S(2)}, u32[]{:S(2)}) collective-permute-start(bf16[16,256,256]{2,1,0:T(8,128)(2,1)} %bitcast.22), channel_id=1, source_target_pairs={{0,1},{1,0},{2,3},{3,2},{4,5},{5,4},{6,7},{7,6},{8,9},{9,8},{10,11... | collective-permute-start | bytes 6291464 | tf_op jit(solution)/shard_map/ppermute | solution.py:168
  10.1 5.0 %collective-permute-start = (bf16[2,64,256]{2,1,0:T(8,128)(2,1)S(1)}, bf16[2,64,256]{2,1,0:T(8,128)(2,1)S(1)}, u32[]{:S(2)}, u32[]{:S(2)}) collective-permute-start(bf16[2,64,256]{2,1,0:T(8,128)(2,1)S(1)} %get-tuple-element.15.own0_ref), channel_id=1, source_target_pairs={{0,8},{2,10},{4,12},{6,14},{8,0},{10,2},{12,4},{14,6},{16,24},{18,... | collective-permute-start | bytes 196616 | tf_op jit(solution)/shard_map/ppermute | solution.py:141
  10.8 5.5 %collective-permute-start.1 = (bf16[2,64,256]{2,1,0:T(8,128)(2,1)S(1)}, bf16[2,64,256]{2,1,0:T(8,128)(2,1)S(1)}, u32[]{:S(2)}, u32[]{:S(2)}) collective-permute-start(bf16[2,64,256]{2,1,0:T(8,128)(2,1)S(1)} %get-tuple-element.15.own0_ref), channel_id=1, source_target_pairs={{16,0},{17,1},{18,2},{19,3},{20,4},{21,5},{22,6},{23,7},{24,8},{25... | collective-permute-start | bytes 196616 | tf_op jit(solution)/shard_map/ppermute | solution.py:141
  16.3 1.3 copy-start.4
  17.6 1.6 %copy-start = (bf16[1,1,16,2,128,256]{5,4,3,2,1,0:T(8,128)(2,1)S(1)}, bf16[1,1,16,2,128,256]{5,4,3,2,1,0:T(8,128)(2,1)}, u32[]{:S(2)}) copy-start(bf16[1,1,16,2,128,256]{5,4,3,2,1,0:T(8,128)(2,1)} %param.9) | copy-start | bytes 6291460
  19.2 1.6 %copy-start.2 = (bf16[1,1,16,2,128,256]{5,4,3,2,1,0:T(8,128)(2,1)S(1)}, bf16[1,1,16,2,128,256]{5,4,3,2,1,0:T(8,128)(2,1)}, u32[]{:S(2)}) copy-start(bf16[1,1,16,2,128,256]{5,4,3,2,1,0:T(8,128)(2,1)} %param.10) | copy-start | bytes 6291460
  20.8 17.1 %copy-start.1 = (bf16[1,1,16,2,128,256]{5,4,3,2,1,0:T(8,128)(2,1)S(1)}, bf16[1,1,16,2,128,256]{5,4,3,2,1,0:T(8,128)(2,1)}, u32[]{:S(2)}) copy-start(bf16[1,1,16,2,128,256]{5,4,3,2,1,0:T(8,128)(2,1)} %param.9) | copy-start | bytes 6291460
  20.8 17.1 %copy-start.3 = (bf16[1,1,16,2,128,256]{5,4,3,2,1,0:T(8,128)(2,1)S(1)}, bf16[1,1,16,2,128,256]{5,4,3,2,1,0:T(8,128)(2,1)}, u32[]{:S(2)}) copy-start(bf16[1,1,16,2,128,256]{5,4,3,2,1,0:T(8,128)(2,1)} %param.10) | copy-start | bytes 6291460
  40.2 20.1 %collective-permute-start.4 = (bf16[2,64,256]{2,1,0:T(8,128)(2,1)S(1)}, bf16[2,64,256]{2,1,0:T(8,128)(2,1)S(1)}, u32[]{:S(2)}, u32[]{:S(2)}) collective-permute-start(bf16[2,64,256]{2,1,0:T(8,128)(2,1)S(1)} %get-tuple-element.8), channel_id=1, source_target_pairs={{0,16},{2,18},{4,20},{6,22},{8,24},{10,26},{12,28},{14,30},{16,32}... | collective-permute-start | bytes 196616 | tf_op jit(solution)/shard_map/ppermute | solution.py:141
  46.0 15.8 %collective-permute-start.5 = (bf16[2,64,256]{2,1,0:T(8,128)(2,1)S(1)}, bf16[2,64,256]{2,1,0:T(8,128)(2,1)S(1)}, u32[]{:S(2)}, u32[]{:S(2)}) collective-permute-start(bf16[2,64,256]{2,1,0:T(8,128)(2,1)S(1)} %get-tuple-element.9), channel_id=1, source_target_pairs={{0,24},{2,26},{4,28},{6,30},{8,16},{10,18},{12,20},{14,22},{16,40}... | collective-permute-start | bytes 196616 | tf_op jit(solution)/shard_map/ppermute | solution.py:141
  79.9 15.7 %collective-permute-start.6 = (bf16[2,64,256]{2,1,0:T(8,128)(2,1)S(1)}, bf16[2,64,256]{2,1,0:T(8,128)(2,1)S(1)}, u32[]{:S(2)}, u32[]{:S(2)}) collective-permute-start(bf16[2,64,256]{2,1,0:T(8,128)(2,1)S(1)} %get-tuple-element.10), channel_id=1, source_target_pairs={{0,16},{2,18},{4,20},{6,22},{8,24},{10,26},{12,28},{14,30},{16,32}... | collective-permute-start | bytes 196616 | tf_op jit(solution)/shard_map/ppermute | solution.py:141
  85.5 14.6 %collective-permute-start.7 = (bf16[2,64,256]{2,1,0:T(8,128)(2,1)S(1)}, bf16[2,64,256]{2,1,0:T(8,128)(2,1)S(1)}, u32[]{:S(2)}, u32[]{:S(2)}) collective-permute-start(bf16[2,64,256]{2,1,0:T(8,128)(2,1)S(1)} %get-tuple-element.11), channel_id=1, source_target_pairs={{0,24},{2,26},{4,28},{6,30},{8,16},{10,18},{12,20},{14,22},{16,40}... | collective-permute-start | bytes 196616 | tf_op jit(solution)/shard_map/ppermute | solution.py:141
  118.3 13.7 %collective-permute-start.8 = (bf16[2,64,256]{2,1,0:T(8,128)(2,1)S(1)}, bf16[2,64,256]{2,1,0:T(8,128)(2,1)S(1)}, u32[]{:S(2)}, u32[]{:S(2)}) collective-permute-start(bf16[2,64,256]{2,1,0:T(8,128)(2,1)S(1)} %get-tuple-element.12), channel_id=1, source_target_pairs={{0,16},{1,9},{2,18},{3,11},{4,20},{5,13},{6,22},{7,15},{8,24},{9,1... | collective-permute-start | bytes 196616 | tf_op jit(solution)/shard_map/ppermute | solution.py:141

commit v2 on v1

--- a/solution.py
+++ b/solution.py
@@ -12,6 +12,8 @@
 PAIR = 2
 ROWS = 64
 HALF = 32
+GROUPS = 4
+LIMIT = 16 * 1024 * 1024
 BF = jnp.bfloat16
 F32 = jnp.float32
 
@@ -40,7 +42,19 @@
     return z * 8 + x * 2 + c
 
 
-def spread_kernel(where_ref, rank_ref, hop_ref, far_ref, own0_ref, far0_ref, next_ref, u0_ref, v0_ref, u1_ref, v1_ref, out_ref):
+def load_kernel(u0, v0, u1, v1, held_ref, sems):
+    copies = [pltpu.make_async_copy(ref, held_ref.at[n], sems.at[n]) for n, ref in enumerate((u0, v0, u1, v1))]
+    for copy in copies:
+        copy.start()
+    for copy in copies:
+        copy.wait()
+
+
+def place_of(j):
+    return (j // 2) % XS, (j // 8) * PAIR + j % 2
+
+
+def spread_kernel(where_ref, rank_ref, far_ref, hop_ref, own0_ref, far0_ref, next_ref, held_ref, out_ref):
     core = where_ref[0]
     z_own = where_ref[1]
     first_layer = where_ref[2] == 0
@@ -61,37 +75,44 @@
         for c in range(PAIR):
             total = next_ref[c].astype(F32) + (hop_ref[c].astype(F32) + far_ref[c].astype(F32))
             traces.append(total.astype(BF))
-        factors = ((1, u0_ref, v0_ref), (0, u1_ref, v1_ref))
-        for x in range(XS):
-            for z in range(2):
-                for c in range(PAIR):
-                    j = block_of(x, z, c)
-                    total = None
-                    for row, u_ref, v_ref in factors:
-                        product = dot_rows(traces[row], u_ref[j])
-                        coef = coefficients(product, rank_ref[row, j])
-                        part = dot_cols(coef, v_ref[j])
-                        total = part if total is None else total + part
-                    out_ref[x, z * PAIR + c] = total.astype(BF)
-
-
-def gather_kernel(where_ref, rank_ref, got_ref, next_ref, u0_ref, v0_ref, u1_ref, v1_ref, hop_ref, far_ref):
+        size = 16 // GROUPS
+        coefs = {}
+        for g in range(GROUPS + 1):
+            for k in range(size):
+                if g < GROUPS:
+                    j = g * size + k
+                    for n, row in ((0, 1), (1, 0)):
+                        product = dot_rows(traces[row], held_ref[2 * n, j])
+                        coefs[n, j] = coefficients(product, rank_ref[row, j])
+                if g > 0:
+                    j = (g - 1) * size + k
+                    total = dot_cols(coefs[0, j], held_ref[1, j]) + dot_cols(coefs[1, j], held_ref[3, j])
+                    x, slot = place_of(j)
+                    out_ref[x, slot] = total.astype(BF)
+
+
+def gather_kernel(where_ref, rank_ref, got_ref, next_ref, held_ref, far_ref, hop_ref):
     core = where_ref[0]
     z_own = where_ref[1]
 
     @pl.when(core == 0)
     def _():
-        factors = ((0, u0_ref, v0_ref), (1, u1_ref, v1_ref))
-        for row, u_ref, v_ref in factors:
-            total = next_ref[row].astype(F32)
-            for x in range(XS):
-                for z in range(2):
-                    for c in range(PAIR):
-                        j = block_of(x, z, c)
-                        product = dot_rows(got_ref[x, z * PAIR + c], v_ref[j])
-                        coef = coefficients(product, rank_ref[row, j])
-                        total = total + dot_cols(coef, u_ref[j])
-            block = total.astype(BF)
+        size = 16 // GROUPS
+        coefs = {}
+        totals = [next_ref[row].astype(F32) for row in range(PAIR)]
+        for g in range(GROUPS + 1):
+            for k in range(size):
+                for row in range(PAIR):
+                    if g < GROUPS:
+                        j = g * size + k
+                        x, slot = place_of(j)
+                        product = dot_rows(got_ref[x, slot], held_ref[2 * row + 1, j])
+                        coefs[row, j] = coefficients(product, rank_ref[row, j])
+                    if g > 0:
+                        j = (g - 1) * size + k
+                        totals[row] = totals[row] + dot_cols(coefs[row, j], held_ref[2 * row, j])
+        for row in range(PAIR):
+            block = totals[row].astype(BF)
             hop_ref[row] = block
             far_ref[row] = block
 
@@ -108,17 +129,50 @@
             far_ref[c] = jnp.where(z_own == 0, sums[1], sums[0])
 
 
+def column(row, size):
+    across = lax.broadcasted_iota(jnp.int32, (size, size), 1)
+    along = lax.broadcasted_iota(jnp.int32, (size, size), 0)
+    picked = jnp.where(across == along, jnp.broadcast_to(row, (size, size)), 0)
+    return jnp.sum(picked, axis=1, keepdims=True)
+
+
+def pack_kernel(layer_ref, source_ref, rank_ref, up_ref, down_ref, packed_ref):
+    layer = layer_ref[0]
+    width = packed_ref.shape[1]
+    sources = jnp.broadcast_to(column(source_ref[...], HALF), (HALF, width))
+    zero = jnp.zeros((HALF, width), BF)
+    for part in range(2):
+        packed_ref[pl.ds(part * HALF, HALF), :] = jnp.where(layer >= sources, up_ref[part], zero)
+        packed_ref[pl.ds(ROWS + part * HALF, HALF), :] = jnp.where(layer <= sources, down_ref[part], zero)
+    ranks = jnp.broadcast_to(column(rank_ref[...], 16), (16, width))
+    packed_ref[pl.ds(2 * ROWS, 16), :] = ranks.astype(F32).astype(BF)
+
+
 def call(kernel, outs, scalars, arrays):
     smem = pl.BlockSpec(memory_space=pltpu.SMEM)
     vmem = pl.BlockSpec(memory_space=pltpu.VMEM)
+    arrays = [pltpu.with_memory_space_constraint(a, pltpu.VMEM) for a in arrays]
     return pl.pallas_call(
         kernel,
         out_shape=outs,
         in_specs=[smem] * len(scalars) + [vmem] * len(arrays),
         out_specs=jax.tree.map(lambda _: vmem, outs),
-        compiler_params=pltpu.CompilerParams(vmem_limit_bytes=48 * 1024 * 1024),
+        compiler_params=pltpu.CompilerParams(vmem_limit_bytes=LIMIT),
         cost_estimate=pl.CostEstimate(flops=64 * 2 * 64 * 256 * 256, bytes_accessed=10 * 1024 * 1024, transcendentals=0),
     )(*scalars, *arrays)
+
+
+def load(own, others):
+    own = [pltpu.with_memory_space_constraint(f, pltpu.HBM) for f in own]
+    return pl.pallas_call(
+        load_kernel,
+        out_shape=pltpu.VMEM((4,) + own[0].shape, BF),
+        in_specs=[pl.BlockSpec(memory_space=pltpu.HBM)] * 2 + [pl.BlockSpec(memory_space=pl.ANY)] * 2,
+        out_specs=pl.BlockSpec(memory_space=pltpu.VMEM),
+        scratch_shapes=[pltpu.SemaphoreType.DMA((4,))],
+        compiler_params=pltpu.CompilerParams(vmem_limit_bytes=LIMIT),
+        cost_estimate=pl.CostEstimate(flops=0, bytes_accessed=8 * 1024 * 1024, transcendentals=0),
+    )(*own, *others)
 
 
 def on_device(layers, up_source, down_source, source_layer, u_factor, v_factor, block_rank):
@@ -149,16 +203,16 @@
     pairs = [[2 * k, 2 * k + 1] for k in range(8)]
     rings = [[block_of(x, z, c) for x in range(XS)] for z in range(2) for c in range(2)]
 
-    up_mask = (layer >= source_layer)[None, :, None]
-    down_mask = (layer <= source_layer)[None, :, None]
-    active_up = jnp.where(up_mask, up_source[0], jnp.zeros_like(up_source[0])).reshape(ROWS, width)
-    active_down = jnp.where(down_mask, down_source[0], jnp.zeros_like(down_source[0])).reshape(ROWS, width)
-    ranks = block_rank[0, 0].astype(BF)
-    rank_rows = jnp.broadcast_to(jnp.pad(ranks, (0, width - ranks.shape[0]))[None, :], (16, width))
-    packed = jnp.concatenate([active_up, active_down, rank_rows], axis=0)
+    vmem = pl.BlockSpec(memory_space=pltpu.VMEM)
+    packed = pl.pallas_call(
+        pack_kernel,
+        out_shape=jax.ShapeDtypeStruct((2 * ROWS + 16, width), BF),
+        in_specs=[pl.BlockSpec(memory_space=pltpu.SMEM)] + [vmem] * 4,
+        out_specs=vmem,
+    )(layer.astype(jnp.int32)[None], source_layer[None], block_rank[0], up_source[0], down_source[0])
     chip = lax.all_gather(packed, "xy", axis=0, axis_index_groups=pairs)
     mine = jnp.where(core == 0, chip[:, :ROWS], chip[:, ROWS : 2 * ROWS])
-    limits = (chip[:, 2 * ROWS, :16].astype(F32) * step).astype(jnp.int32)
+    limits = (chip[:, 2 * ROWS :, 0].astype(F32) * step).astype(jnp.int32)
 
     u_own = u_factor[0, 0].reshape(16, 2 * max_rank, width)
     v_own = v_factor[0, 0].reshape(16, 2 * max_rank, width)
@@ -169,16 +223,16 @@
 
     where = jnp.stack([core, z_own, layer]).astype(jnp.int32)
     scalars = (where, limits)
-    factors = (u_own, v_own, u_other, v_other)
+    held = load((u_own, v_own), (u_other, v_other))
     pair_shape = jax.ShapeDtypeStruct((PAIR, ROWS, width), BF)
     ring_shape = jax.ShapeDtypeStruct((XS, 2 * PAIR, ROWS, width), BF)
 
     hop = jnp.where(core == 0, mine, jnp.zeros_like(mine))
     far = far0
     for sweep in range(STEPS):
-        sent = call(spread_kernel, ring_shape, scalars, (hop, far, mine, far0, following) + factors)
+        sent = call(spread_kernel, ring_shape, scalars, (far, hop, mine, far0, following, held))
         got = lax.all_to_all(sent, "xy", 0, 0, axis_index_groups=rings)
-        near, away = call(gather_kernel, (pair_shape, pair_shape), scalars, (got, following) + factors)
+        away, near = call(gather_kernel, (pair_shape, pair_shape), scalars, (got, following, held))
         if sweep < STEPS - 1:
             far = send(away, ahead_far)
             hop = send(near, ahead)

time: 146 us -> 127 us (0.87)
  Pallas kernels: 25.6 us -> 14.4 us
  starting transfers between devices: 56 us -> 47.6 us
  local copies, waits for them, and re-layouts: 4.71 us -> 0.01 us
  waiting for transfers between devices: 10.1 us -> 14.5 us
  blocking collectives: 45.6 us -> 48.4 us
  other arithmetic: 2.95 us -> 0.88 us
    pallas_call x6, Pallas kernels: 25.6 us -> 9.88 us  [call(): pl.pallas_call(kernel, out_shape=outs, in_specs=[smem] * len(scalars) + [...]
    ppermute x7, starting transfers between devices: 51.5 us -> 43.1 us  [send(): return lax.ppermute(block, both, route)]
    unnamed x10 -> x0, local copies, waits for them, and re-layouts: 4.5 us -> none
    pallas_call x0 -> x2, Pallas kernels: none -> 4.48 us  [the longest x1 2.94 us: load(): pl.pallas_call(load_kernel, out_shape=pltpu.VMEM((4,) + own[0].shape, BF)...]
    ppermute x7, waiting for transfers between devices: 10.1 us -> 14.5 us  [send(): return lax.ppermute(block, both, route)]
    all_gather x1, blocking collectives: 13.1 us -> 14.8 us  [on_device(): lax.all_gather(final[1 - core], 'xy', axis=0, axis_index_groups=pairs)]
  transfers between devices with their start and end apart: 9 -> 9, of which waited for: 4 -> 5; matrix products, arithmetic and copies ran while one was open for 2% -> 0% of each run, Pallas kernels for 0% -> 4%
where the time goes in v2:
time: 127 us
  blocking collectives  48.4 us (38%)
  starting transfers between devices  47.6 us (37%)
  waiting for transfers between devices  14.5 us (11%)
  Pallas kernels  14.4 us (11%)
    ppermute x7, starting transfers between devices, send(): return lax.ppermute(block, both, route)  43.1 us
    all_to_all x3, blocking collectives, on_device(): got = lax.all_to_all(sent, 'xy', 0, 0, axis_index_groups=rings)  30 us
    all_gather x1, blocking collectives, on_device(): lax.all_gather(final[1 - core], 'xy', axis=0, axis_index_groups=pairs)  14.8 us
    ppermute x7, waiting for transfers between devices, send(): return lax.ppermute(block, both, route)  14.5 us
    pallas_call x6, Pallas kernels, call(): pl.pallas_call(kernel, out_shape=outs, in_specs=[smem] * len(scalars) + [...  9.88 us
    all_gather x1, blocking collectives, on_device(): chip = lax.all_gather(packed, 'xy', axis=0, axis_index_groups=pairs)  3.59 us
    pallas_call x1, Pallas kernels, load(): pl.pallas_call(load_kernel, out_shape=pltpu.VMEM((4,) + own[0].shape, BF)...  2.94 us
    ppermute x1, starting transfers between devices, on_device(): u_other = lax.ppermute(u_own, 'xy', [(i, i ^ 1) for i in range(16)])  2.59 us
  transfers between devices with their start and end apart: 9, of which 5 were waited for; matrix products, arithmetic and copies ran while one was open for 0% of the time, Pallas kernels for 4%

profile of v2, /device:TPU:33, one launch (start us, length us, event | category | flops | bytes accessed | tf_op | source)
XLA Modules:
  0.0 126.6 jit_solution(12587208141261056403)
XLA Ops:
  0.6 2.6 %collective-permute-start.2 = (bf16[16,256,256]{2,1,0:T(8,128)(2,1)}, bf16[16,256,256]{2,1,0:T(8,128)(2,1)S(1)}, u32[]{:S(2)}, u32[]{:S(2)}) collective-permute-start(bf16[16,256,256]{2,1,0:T(8,128)(2,1)} %bitcast.12), channel_id=1, source_target_pairs={{0,1},{1,0},{2,3},{3,2},{4,5},{5,4},{6,7},{7,6},{8,9},{9,8},{10,11... | collective-permute-start | bytes 6291464 | tf_op jit(solution)/shard_map/ppermute | solution.py:221
  3.2 1.9 %collective-permute-start.3 = (bf16[16,256,256]{2,1,0:T(8,128)(2,1)}, bf16[16,256,256]{2,1,0:T(8,128)(2,1)}, u32[]{:S(2)}, u32[]{:S(2)}) collective-permute-start(bf16[16,256,256]{2,1,0:T(8,128)(2,1)} %bitcast.14), channel_id=1, source_target_pairs={{0,1},{1,0},{2,3},{3,2},{4,5},{5,4},{6,7},{7,6},{8,9},{9,8},{10,11... | collective-permute-start | bytes 6291464 | tf_op jit(solution)/shard_map/ppermute | solution.py:222
  5.2 1.5 %shard_map.77 = bf16[144,256]{1,0:T(8,128)(2,1)} custom-call(s32[1]{0:T(128)} %bitcast.layer_ref, s32[1,32]{1,0:T(1,128)} %bitcast.22, s32[1,16]{1,0:T(1,128)} %bitcast.23, bf16[2,32,256]{2,1,0:T(8,128)(2,1)} %bitcast.18, bf16[2,32,256]{2,1,0:T(8,128)(2,1)} %bitcast.19), custom_call_target="tpu_custom_call" | custom-call | tf_op jit(solution)/shard_map/pallas_call | solution.py:207
  6.7 3.6 %all-gather = bf16[288,256]{1,0:T(8,128)(2,1)S(1)} all-gather(bf16[144,256]{1,0:T(8,128)(2,1)} %shard_map.77), channel_id=2, replica_groups={{0,1},{2,3},{4,5},{6,7},{8,9},{10,11},{12,13},{14,15},{16,17},{18,19},{..., dimensions={0}, use_global_device_ids=true | all-gather | bytes 221184 | tf_op jit(solution)/shard_map/all_gather | solution.py:213
  10.3 0.7 collective-permute-start
  11.0 4.2 %collective-permute-start.1 = (bf16[2,64,256]{2,1,0:T(8,128)(2,1)S(1)}, bf16[2,64,256]{2,1,0:T(8,128)(2,1)S(1)}, u32[]{:S(2)}, u32[]{:S(2)}) collective-permute-start(bf16[2,64,256]{2,1,0:T(8,128)(2,1)S(1)} %get-tuple-element.15.own0_ref), channel_id=1, source_target_pairs={{16,0},{17,1},{18,2},{19,3},{20,4},{21,5},{22,6},{23,7},{24,8},{25... | collective-permute-start | bytes 196616 | tf_op jit(solution)/shard_map/ppermute | solution.py:195
  15.2 0.1 convert_reduce_fusion.rank_ref
  15.3 0.1 pad_add_fusion.where_ref
  15.4 0.0 collective-permute-done.2.u1
  15.4 0.0 collective-permute-done.3.v1
  15.4 2.9 %shard_map.78.held_ref = bf16[4,16,256,256]{3,2,1,0:T(8,128)(2,1)S(1)} custom-call(bf16[16,256,256]{2,1,0:T(8,128)(2,1)} %bitcast.13, bf16[16,256,256]{2,1,0:T(8,128)(2,1)} %bitcast.15, bf16[16,256,256]{2,1,0:T(8,128)(2,1)S(1)} %collective-permute-done.2.u1, bf16[16,256,256]{2,1,0:T(8,128)(2,1)} %collective-permute-done.3.v1), custom_call_target="tpu_custom_call" | custom-call | bytes 8388608 | tf_op jit(solution)/shard_map/pallas_call | solution.py:167
  18.3 0.0 collective-permute-done.far_ref.far0_ref
  18.4 0.0 collective-permute-done.1.next_ref
  18.4 2.7 %shard_map.79 = bf16[4,4,64,256]{3,2,1,0:T(8,128)(2,1)S(1)} custom-call(s32[3]{0:T(128)S(1)} %pad_add_fusion.where_ref, s32[2,16]{1,0:T(2,128)S(1)} %convert_reduce_fusion.rank_ref, bf16[2,64,256]{2,1,0:T(8,128)(2,1)S(1)} %collective-permute-done.far_ref.far0_ref, bf16[2,64,256]{2,1,0:T(8,128)(2,1)S(1)} %get-tuple-element.14.hop_ref, ...), custom_call_target="tpu_custom_call" | custom-call | flops 536870912 | bytes 10485760 | tf_op jit(solution)/shard_map/pallas_call | solution.py:155
  21.0 10.8 %all_to_all.15.got_ref = bf16[4,4,64,256]{3,2,1,0:T(8,128)(2,1)S(1)} all-to-all(bf16[4,4,64,256]{3,2,1,0:T(8,128)(2,1)S(1)} %shard_map.79), channel_id=1, replica_groups={{0,2,4,6},{1,3,5,7},{8,10,12,14},{9,11,13,15},{16,18,20,22},{17,19,21,2..., dimensions={0} | all-to-all | bytes 1048576 | tf_op jit(solution)/shard_map/all_to_all | solution.py:234
  31.8 0.6 shard_map.80
  32.4 16.3 %collective-permute-start.4 = (bf16[2,64,256]{2,1,0:T(8,128)(2,1)S(1)}, bf16[2,64,256]{2,1,0:T(8,128)(2,1)S(1)}, u32[]{:S(2)}, u32[]{:S(2)}) collective-permute-start(bf16[2,64,256]{2,1,0:T(8,128)(2,1)S(1)} %get-tuple-element.8), channel_id=1, source_target_pairs={{0,24},{2,26},{4,28},{6,30},{8,16},{10,18},{12,20},{14,22},{16,40}... | collective-permute-start | bytes 196616 | tf_op jit(solution)/shard_map/ppermute | solution.py:195
  48.7 1.9 %collective-permute-start.5 = (bf16[2,64,256]{2,1,0:T(8,128)(2,1)S(1)}, bf16[2,64,256]{2,1,0:T(8,128)(2,1)S(1)}, u32[]{:S(2)}, u32[]{:S(2)}) collective-permute-start(bf16[2,64,256]{2,1,0:T(8,128)(2,1)S(1)} %get-tuple-element.9), channel_id=1, source_target_pairs={{0,16},{2,18},{4,20},{6,22},{8,24},{10,26},{12,28},{14,30},{16,32}... | collective-permute-start | bytes 196616 | tf_op jit(solution)/shard_map/ppermute | solution.py:195
  50.6 1.6 %collective-permute-done.4.far_ref = bf16[2,64,256]{2,1,0:T(8,128)(2,1)S(1)} collective-permute-done((bf16[2,64,256]{2,1,0:T(8,128)(2,1)S(1)}, bf16[2,64,256]{2,1,0:T(8,128)(2,1)S(1)}, u32[]{:S(2)}, u32[]{:S(2)}) %collective-permute-start.4) | collective-permute-done | bytes 65568 | tf_op jit(solution)/shard_map/ppermute | solution.py:195
  52.3 1.4 %collective-permute-done.5.hop_ref = bf16[2,64,256]{2,1,0:T(8,128)(2,1)S(1)} collective-permute-done((bf16[2,64,256]{2,1,0:T(8,128)(2,1)S(1)}, bf16[2,64,256]{2,1,0:T(8,128)(2,1)S(1)}, u32[]{:S(2)}, u32[]{:S(2)}) %collective-permute-start.5) | collective-permute-done | bytes 65568 | tf_op jit(solution)/shard_map/ppermute | solution.py:195
  53.7 2.7 %shard_map.81 = bf16[4,4,64,256]{3,2,1,0:T(8,128)(2,1)S(1)} custom-call(s32[3]{0:T(128)S(1)} %pad_add_fusion.where_ref, s32[2,16]{1,0:T(2,128)S(1)} %convert_reduce_fusion.rank_ref, bf16[2,64,256]{2,1,0:T(8,128)(2,1)S(1)} %collective-permute-done.4.far_ref, bf16[2,64,256]{2,1,0:T(8,128)(2,1)S(1)} %collective-permute-done.5.hop_ref, ...), custom_call_target="tpu_custom_call" | custom-call | flops 536870912 | bytes 10485760 | tf_op jit(solution)/shard_map/pallas_call | solution.py:155
  56.4 9.6 %all_to_all.16.got_ref = bf16[4,4,64,256]{3,2,1,0:T(8,128)(2,1)S(1)} all-to-all(bf16[4,4,64,256]{3,2,1,0:T(8,128)(2,1)S(1)} %shard_map.81), channel_id=1, replica_groups={{0,2,4,6},{1,3,5,7},{8,10,12,14},{9,11,13,15},{16,18,20,22},{17,19,21,2..., dimensions={0} | all-to-all | bytes 1048576 | tf_op jit(solution)/shard_map/all_to_all | solution.py:234
  66.0 0.6 shard_map.82
  66.7 12.0 %collective-permute-start.6 = (bf16[2,64,256]{2,1,0:T(8,128)(2,1)S(1)}, bf16[2,64,256]{2,1,0:T(8,128)(2,1)S(1)}, u32[]{:S(2)}, u32[]{:S(2)}) collective-permute-start(bf16[2,64,256]{2,1,0:T(8,128)(2,1)S(1)} %get-tuple-element.10), channel_id=1, source_target_pairs={{0,24},{2,26},{4,28},{6,30},{8,16},{10,18},{12,20},{14,22},{16,40}... | collective-permute-start | bytes 196616 | tf_op jit(solution)/shard_map/ppermute | solution.py:195
  78.7 1.9 %collective-permute-start.7 = (bf16[2,64,256]{2,1,0:T(8,128)(2,1)S(1)}, bf16[2,64,256]{2,1,0:T(8,128)(2,1)S(1)}, u32[]{:S(2)}, u32[]{:S(2)}) collective-permute-start(bf16[2,64,256]{2,1,0:T(8,128)(2,1)S(1)} %get-tuple-element.11), channel_id=1, source_target_pairs={{0,16},{2,18},{4,20},{6,22},{8,24},{10,26},{12,28},{14,30},{16,32}... | collective-permute-start | bytes 196616 | tf_op jit(solution)/shard_map/ppermute | solution.py:195
  80.6 0.7 collective-permute-done.6.far_ref
  81.3 2.3 %collective-permute-done.7.hop_ref = bf16[2,64,256]{2,1,0:T(8,128)(2,1)S(1)} collective-permute-done((bf16[2,64,256]{2,1,0:T(8,128)(2,1)S(1)}, bf16[2,64,256]{2,1,0:T(8,128)(2,1)S(1)}, u32[]{:S(2)}, u32[]{:S(2)}) %collective-permute-start.7) | collective-permute-done | bytes 65568 | tf_op jit(solution)/shard_map/ppermute | solution.py:195
  83.7 2.7 %shard_map.83 = bf16[4,4,64,256]{3,2,1,0:T(8,128)(2,1)S(1)} custom-call(s32[3]{0:T(128)S(1)} %pad_add_fusion.where_ref, s32[2,16]{1,0:T(2,128)S(1)} %convert_reduce_fusion.rank_ref, bf16[2,64,256]{2,1,0:T(8,128)(2,1)S(1)} %collective-permute-done.6.far_ref, bf16[2,64,256]{2,1,0:T(8,128)(2,1)S(1)} %collective-permute-done.7.hop_ref, ...), custom_call_target="tpu_custom_call" | custom-call | flops 536870912 | bytes 10485760 | tf_op jit(solution)/shard_map/pallas_call | solution.py:155
  86.3 9.6 %all_to_all.17.got_ref = bf16[4,4,64,256]{3,2,1,0:T(8,128)(2,1)S(1)} all-to-all(bf16[4,4,64,256]{3,2,1,0:T(8,128)(2,1)S(1)} %shard_map.83), channel_id=1, replica_groups={{0,2,4,6},{1,3,5,7},{8,10,12,14},{9,11,13,15},{16,18,20,22},{17,19,21,2..., dimensions={0} | all-to-all | bytes 1048576 | tf_op jit(solution)/shard_map/all_to_all | solution.py:234
  96.0 0.6 shard_map.84
  96.6 6.1 %collective-permute-start.8 = (bf16[2,64,256]{2,1,0:T(8,128)(2,1)S(1)}, bf16[2,64,256]{2,1,0:T(8,128)(2,1)S(1)}, u32[]{:S(2)}, u32[]{:S(2)}) collective-permute-start(bf16[2,64,256]{2,1,0:T(8,128)(2,1)S(1)} %get-tuple-element.12), channel_id=1, source_target_pairs={{0,16},{1,9},{2,18},{3,11},{4,20},{5,13},{6,22},{7,15},{8,24},{9,1... | collective-permute-start | bytes 196616 | tf_op jit(solution)/shard_map/ppermute | solution.py:195
  102.7 8.3 %collective-permute-done.8 = bf16[2,64,256]{2,1,0:T(8,128)(2,1)S(1)} collective-permute-done((bf16[2,64,256]{2,1,0:T(8,128)(2,1)S(1)}, bf16[2,64,256]{2,1,0:T(8,128)(2,1)S(1)}, u32[]{:S(2)}, u32[]{:S(2)}) %collective-permute-start.8) | collective-permute-done | bytes 65568 | tf_op jit(solution)/shard_map/ppermute | solution.py:195
  111.1 14.8 %all_gather.11 = bf16[2,64,256]{2,1,0:T(8,128)(2,1)S(1)} all-gather(bf16[1,64,256]{2,1,0:T(8,128)(2,1)S(1)} %constant_dynamic-slice_fusion), channel_id=1, replica_groups={{0,1},{2,3},{4,5},{6,7},{8,9},{10,11},{12,13},{14,15},{16,17},{18,19},{..., dimensions={0}, use_global_device_ids=true | all-gather | bytes 98304 | tf_op jit(solution)/shard_map/all_gather | solution.py:244
  125.9 0.6 broadcast_select_fusion.1
  (3 shorter events, 0.1 us)
Async XLA Ops:
  0.6 14.8 %collective-permute-start.2 = (bf16[16,256,256]{2,1,0:T(8,128)(2,1)}, bf16[16,256,256]{2,1,0:T(8,128)(2,1)S(1)}, u32[]{:S(2)}, u32[]{:S(2)}) collective-permute-start(bf16[16,256,256]{2,1,0:T(8,128)(2,1)} %bitcast.12), channel_id=1, source_target_pairs={{0,1},{1,0},{2,3},{3,2},{4,5},{5,4},{6,7},{7,6},{8,9},{9,8},{10,11... | collective-permute-start | bytes 6291464 | tf_op jit(solution)/shard_map/ppermute | solution.py:221
  3.2 12.2 %collective-permute-start.3 = (bf16[16,256,256]{2,1,0:T(8,128)(2,1)}, bf16[16,256,256]{2,1,0:T(8,128)(2,1)}, u32[]{:S(2)}, u32[]{:S(2)}) collective-permute-start(bf16[16,256,256]{2,1,0:T(8,128)(2,1)} %bitcast.14), channel_id=1, source_target_pairs={{0,1},{1,0},{2,3},{3,2},{4,5},{5,4},{6,7},{7,6},{8,9},{9,8},{10,11... | collective-permute-start | bytes 6291464 | tf_op jit(solution)/shard_map/ppermute | solution.py:222
  10.3 8.0 %collective-permute-start = (bf16[2,64,256]{2,1,0:T(8,128)(2,1)S(1)}, bf16[2,64,256]{2,1,0:T(8,128)(2,1)S(1)}, u32[]{:S(2)}, u32[]{:S(2)}) collective-permute-start(bf16[2,64,256]{2,1,0:T(8,128)(2,1)S(1)} %get-tuple-element.15.own0_ref), channel_id=1, source_target_pairs={{0,8},{2,10},{4,12},{6,14},{8,0},{10,2},{12,4},{14,6},{16,24},{18,... | collective-permute-start | bytes 196616 | tf_op jit(solution)/shard_map/ppermute | solution.py:195
  11.0 7.4 %collective-permute-start.1 = (bf16[2,64,256]{2,1,0:T(8,128)(2,1)S(1)}, bf16[2,64,256]{2,1,0:T(8,128)(2,1)S(1)}, u32[]{:S(2)}, u32[]{:S(2)}) collective-permute-start(bf16[2,64,256]{2,1,0:T(8,128)(2,1)S(1)} %get-tuple-element.15.own0_ref), channel_id=1, source_target_pairs={{16,0},{17,1},{18,2},{19,3},{20,4},{21,5},{22,6},{23,7},{24,8},{25... | collective-permute-start | bytes 196616 | tf_op jit(solution)/shard_map/ppermute | solution.py:195
  32.4 19.9 %collective-permute-start.4 = (bf16[2,64,256]{2,1,0:T(8,128)(2,1)S(1)}, bf16[2,64,256]{2,1,0:T(8,128)(2,1)S(1)}, u32[]{:S(2)}, u32[]{:S(2)}) collective-permute-start(bf16[2,64,256]{2,1,0:T(8,128)(2,1)S(1)} %get-tuple-element.8), channel_id=1, source_target_pairs={{0,24},{2,26},{4,28},{6,30},{8,16},{10,18},{12,20},{14,22},{16,40}... | collective-permute-start | bytes 196616 | tf_op jit(solution)/shard_map/ppermute | solution.py:195
  48.7 5.0 %collective-permute-start.5 = (bf16[2,64,256]{2,1,0:T(8,128)(2,1)S(1)}, bf16[2,64,256]{2,1,0:T(8,128)(2,1)S(1)}, u32[]{:S(2)}, u32[]{:S(2)}) collective-permute-start(bf16[2,64,256]{2,1,0:T(8,128)(2,1)S(1)} %get-tuple-element.9), channel_id=1, source_target_pairs={{0,16},{2,18},{4,20},{6,22},{8,24},{10,26},{12,28},{14,30},{16,32}... | collective-permute-start | bytes 196616 | tf_op jit(solution)/shard_map/ppermute | solution.py:195
  66.7 14.7 %collective-permute-start.6 = (bf16[2,64,256]{2,1,0:T(8,128)(2,1)S(1)}, bf16[2,64,256]{2,1,0:T(8,128)(2,1)S(1)}, u32[]{:S(2)}, u32[]{:S(2)}) collective-permute-start(bf16[2,64,256]{2,1,0:T(8,128)(2,1)S(1)} %get-tuple-element.10), channel_id=1, source_target_pairs={{0,24},{2,26},{4,28},{6,30},{8,16},{10,18},{12,20},{14,22},{16,40}... | collective-permute-start | bytes 196616 | tf_op jit(solution)/shard_map/ppermute | solution.py:195
  78.7 5.0 %collective-permute-start.7 = (bf16[2,64,256]{2,1,0:T(8,128)(2,1)S(1)}, bf16[2,64,256]{2,1,0:T(8,128)(2,1)S(1)}, u32[]{:S(2)}, u32[]{:S(2)}) collective-permute-start(bf16[2,64,256]{2,1,0:T(8,128)(2,1)S(1)} %get-tuple-element.11), channel_id=1, source_target_pairs={{0,16},{2,18},{4,20},{6,22},{8,24},{10,26},{12,28},{14,30},{16,32}... | collective-permute-start | bytes 196616 | tf_op jit(solution)/shard_map/ppermute | solution.py:195
  96.6 14.4 %collective-permute-start.8 = (bf16[2,64,256]{2,1,0:T(8,128)(2,1)S(1)}, bf16[2,64,256]{2,1,0:T(8,128)(2,1)S(1)}, u32[]{:S(2)}, u32[]{:S(2)}) collective-permute-start(bf16[2,64,256]{2,1,0:T(8,128)(2,1)S(1)} %get-tuple-element.12), channel_id=1, source_target_pairs={{0,16},{1,9},{2,18},{3,11},{4,20},{5,13},{6,22},{7,15},{8,24},{9,1... | collective-permute-start | bytes 196616 | tf_op jit(solution)/shard_map/ppermute | solution.py:195

commit v3 on v2

--- a/solution.py
+++ b/solution.py
@@ -13,6 +13,7 @@
 ROWS = 64
 HALF = 32
 GROUPS = 4
+SIZE = 4
 LIMIT = 16 * 1024 * 1024
 BF = jnp.bfloat16
 F32 = jnp.float32
@@ -54,63 +55,89 @@
     return (j // 2) % XS, (j // 8) * PAIR + j % 2
 
 
-def spread_kernel(where_ref, rank_ref, far_ref, hop_ref, own0_ref, far0_ref, next_ref, held_ref, out_ref):
+def added(*refs):
+    total = refs[0].astype(F32)
+    for ref in refs[1:]:
+        total = total + ref.astype(F32)
+    return total.astype(BF)
+
+
+def spread(where_ref, rank_ref, own, far, down, held_ref, out_ref):
     core = where_ref[0]
     z_own = where_ref[1]
-    first_layer = where_ref[2] == 0
 
     @pl.when(core == 0)
     def _():
         for c in range(PAIR):
-            own = jnp.where(first_layer, own0_ref[c], hop_ref[c])
-            far = jnp.where(first_layer, far0_ref[c], far_ref[c])
+            near_block = own(c)
+            far_block = far(c)
             for z in range(2):
-                block = jnp.where(z_own == z, own, far)
+                block = jnp.where(z_own == z, near_block, far_block)
                 for x in range(XS):
                     out_ref[x, z * PAIR + c] = block
 
     @pl.when(core == 1)
     def _():
-        traces = []
-        for c in range(PAIR):
-            total = next_ref[c].astype(F32) + (hop_ref[c].astype(F32) + far_ref[c].astype(F32))
-            traces.append(total.astype(BF))
-        size = 16 // GROUPS
+        traces = [down(c) for c in range(PAIR)]
         coefs = {}
         for g in range(GROUPS + 1):
-            for k in range(size):
+            for k in range(SIZE):
                 if g < GROUPS:
-                    j = g * size + k
-                    for n, row in ((0, 1), (1, 0)):
-                        product = dot_rows(traces[row], held_ref[2 * n, j])
-                        coefs[n, j] = coefficients(product, rank_ref[row, j])
+                    j = g * SIZE + k
+                    for n in range(PAIR):
+                        product = dot_rows(traces[1 - n], held_ref[2 * n, j])
+                        coefs[n, j] = coefficients(product, rank_ref[1 - n, j])
                 if g > 0:
-                    j = (g - 1) * size + k
+                    j = (g - 1) * SIZE + k
                     total = dot_cols(coefs[0, j], held_ref[1, j]) + dot_cols(coefs[1, j], held_ref[3, j])
                     x, slot = place_of(j)
                     out_ref[x, slot] = total.astype(BF)
 
 
-def gather_kernel(where_ref, rank_ref, got_ref, next_ref, held_ref, far_ref, hop_ref):
+def first_spread_kernel(where_ref, rank_ref, own0_ref, far0_ref, next_ref, held_ref, out_ref):
+    spread(
+        where_ref,
+        rank_ref,
+        lambda c: own0_ref[c],
+        lambda c: far0_ref[c],
+        lambda c: next_ref[c],
+        held_ref,
+        out_ref,
+    )
+
+
+def spread_kernel(where_ref, rank_ref, far_ref, hop_ref, own0_ref, far0_ref, next_ref, held_ref, out_ref):
+    spread(
+        where_ref,
+        rank_ref,
+        lambda c: added(own0_ref[c], hop_ref[c]),
+        lambda c: added(far0_ref[c], far_ref[c]),
+        lambda c: added(next_ref[c], hop_ref[c], far_ref[c]),
+        held_ref,
+        out_ref,
+    )
+
+
+def gather_kernel(where_ref, rank_ref, got_ref, held_ref, far_ref, hop_ref):
     core = where_ref[0]
     z_own = where_ref[1]
 
     @pl.when(core == 0)
     def _():
-        size = 16 // GROUPS
+        totals = [None, None]
         coefs = {}
-        totals = [next_ref[row].astype(F32) for row in range(PAIR)]
         for g in range(GROUPS + 1):
-            for k in range(size):
+            for k in range(SIZE):
                 for row in range(PAIR):
                     if g < GROUPS:
-                        j = g * size + k
+                        j = g * SIZE + k
                         x, slot = place_of(j)
                         product = dot_rows(got_ref[x, slot], held_ref[2 * row + 1, j])
                         coefs[row, j] = coefficients(product, rank_ref[row, j])
                     if g > 0:
-                        j = (g - 1) * size + k
-                        totals[row] = totals[row] + dot_cols(coefs[row, j], held_ref[2 * row, j])
+                        j = (g - 1) * SIZE + k
+                        part = dot_cols(coefs[row, j], held_ref[2 * row, j])
+                        totals[row] = part if totals[row] is None else totals[row] + part
         for row in range(PAIR):
             block = totals[row].astype(BF)
             hop_ref[row] = block
@@ -206,41 +233,40 @@
     vmem = pl.BlockSpec(memory_space=pltpu.VMEM)
     packed = pl.pallas_call(
         pack_kernel,
-        out_shape=jax.ShapeDtypeStruct((2 * ROWS + 16, width), BF),
+        out_shape=pltpu.VMEM((2 * ROWS + 16, width), BF),
         in_specs=[pl.BlockSpec(memory_space=pltpu.SMEM)] + [vmem] * 4,
         out_specs=vmem,
     )(layer.astype(jnp.int32)[None], source_layer[None], block_rank[0], up_source[0], down_source[0])
     chip = lax.all_gather(packed, "xy", axis=0, axis_index_groups=pairs)
+    u_own = u_factor[0, 0].reshape(16, 2 * max_rank, width)
+    v_own = v_factor[0, 0].reshape(16, 2 * max_rank, width)
+    u_sent, v_sent, chip = lax.optimization_barrier((u_own, v_own, chip))
+    u_other = lax.ppermute(u_sent, "xy", [(i, i ^ 1) for i in range(16)])
+    v_other = lax.ppermute(v_sent, "xy", [(i, i ^ 1) for i in range(16)])
     mine = jnp.where(core == 0, chip[:, :ROWS], chip[:, ROWS : 2 * ROWS])
     limits = (chip[:, 2 * ROWS :, 0].astype(F32) * step).astype(jnp.int32)
-
-    u_own = u_factor[0, 0].reshape(16, 2 * max_rank, width)
-    v_own = v_factor[0, 0].reshape(16, 2 * max_rank, width)
     far0 = send(mine, lambda l, i: (l, i ^ 8) if i % 2 == 0 else None)
-    following = send(mine, lambda l, i: (l - 1, i))
-    u_other = lax.ppermute(u_own, "xy", [(i, i ^ 1) for i in range(16)])
-    v_other = lax.ppermute(v_own, "xy", [(i, i ^ 1) for i in range(16)])
-
+    following = send(mine, lambda l, i: (l - 1, i) if i % 2 == 1 else None)
     where = jnp.stack([core, z_own, layer]).astype(jnp.int32)
     scalars = (where, limits)
     held = load((u_own, v_own), (u_other, v_other))
     pair_shape = jax.ShapeDtypeStruct((PAIR, ROWS, width), BF)
     ring_shape = jax.ShapeDtypeStruct((XS, 2 * PAIR, ROWS, width), BF)
 
-    hop = jnp.where(core == 0, mine, jnp.zeros_like(mine))
-    far = far0
     for sweep in range(STEPS):
-        sent = call(spread_kernel, ring_shape, scalars, (far, hop, mine, far0, following, held))
+        if sweep == 0:
+            sent = call(first_spread_kernel, ring_shape, scalars, (mine, far0, following, held))
+        else:
+            sent = call(spread_kernel, ring_shape, scalars, (far, hop, mine, far0, following, held))
         got = lax.all_to_all(sent, "xy", 0, 0, axis_index_groups=rings)
-        away, near = call(gather_kernel, (pair_shape, pair_shape), scalars, (got, following, held))
+        away, near = call(gather_kernel, (pair_shape, pair_shape), scalars, (got, held))
         if sweep < STEPS - 1:
             far = send(away, ahead_far)
             hop = send(near, ahead)
 
     last = send(away, lambda l, i: (l + 1, i) if i % 2 == 0 else (l, i ^ 8))
-    up_pair = jnp.where(layer == 0, mine, last)
-    down_pair = (mine.astype(F32) + (near.astype(F32) + last.astype(F32))).astype(BF)
-    final = jnp.where(core == 0, up_pair, down_pair)
+    kept_sum = jnp.where(core == 0, jnp.zeros_like(near), near)
+    final = (mine.astype(F32) + (kept_sum.astype(F32) + last.astype(F32))).astype(BF)
     swapped = lax.all_gather(final[1 - core], "xy", axis=0, axis_index_groups=pairs)
     kept = final[core]
     other = swapped[1 - core]

time: 127 us -> 120 us (0.945)
  the two profiles are of different devices: /device:TPU:33 before, /device:TPU:65 now
where the time goes in v3:
time: 120 us
  starting transfers between devices  49.7 us (41%)
  blocking collectives  42.5 us (35%)
  Pallas kernels  13.7 us (11%)
  waiting for transfers between devices  12.2 us (10%)
    ppermute x7, starting transfers between devices, send(): return lax.ppermute(block, both, route)  45.4 us
    all_to_all x3, blocking collectives, on_device(): got = lax.all_to_all(sent, 'xy', 0, 0, axis_index_groups=rings)  29.7 us
    ppermute x7, waiting for transfers between devices, send(): return lax.ppermute(block, both, route)  12.2 us
    all_gather x1, blocking collectives, on_device(): lax.all_gather(final[1 - core], 'xy', axis=0, axis_index_groups=pairs)  10.5 us
    pallas_call x6, Pallas kernels, call(): pl.pallas_call(kernel, out_shape=outs, in_specs=[smem] * len(scalars) + [...  9.88 us
    pallas_call x1, Pallas kernels, load(): pl.pallas_call(load_kernel, out_shape=pltpu.VMEM((4,) + own[0].shape, BF)...  2.94 us
  transfers between devices with their start and end apart: 9, of which 4 were waited for; matrix products, arithmetic and copies ran while one was open for 0% of the time, Pallas kernels for 2%

profile of v3, /device:TPU:65, one launch (start us, length us, event | category | flops | bytes accessed | tf_op | source)
XLA Modules:
  0.0 119.9 jit_solution(5717158704542232037)
XLA Ops:
  0.6 0.9 shard_map.77
  1.5 2.2 %all-gather = bf16[288,256]{1,0:T(8,128)(2,1)S(1)} all-gather(bf16[144,256]{1,0:T(8,128)(2,1)S(1)} %shard_map.77), channel_id=2, replica_groups={{0,1},{2,3},{4,5},{6,7},{8,9},{10,11},{12,13},{14,15},{16,17},{18,19},{..., dimensions={0}, use_global_device_ids=true | all-gather | bytes 221184 | tf_op jit(solution)/shard_map/all_gather | solution.py:240
  3.8 2.3 %collective-permute-start.2 = (bf16[16,256,256]{2,1,0:T(8,128)(2,1)}, bf16[16,256,256]{2,1,0:T(8,128)(2,1)S(1)}, u32[]{:S(2)}, u32[]{:S(2)}) collective-permute-start(bf16[16,256,256]{2,1,0:T(8,128)(2,1)} %bitcast.12), channel_id=1, source_target_pairs={{0,1},{1,0},{2,3},{3,2},{4,5},{5,4},{6,7},{7,6},{8,9},{9,8},{10,11... | collective-permute-start | bytes 6291464 | tf_op jit(solution)/shard_map/ppermute | solution.py:244
  6.0 2.1 %collective-permute-start.3 = (bf16[16,256,256]{2,1,0:T(8,128)(2,1)}, bf16[16,256,256]{2,1,0:T(8,128)(2,1)}, u32[]{:S(2)}, u32[]{:S(2)}) collective-permute-start(bf16[16,256,256]{2,1,0:T(8,128)(2,1)} %bitcast.14), channel_id=1, source_target_pairs={{0,1},{1,0},{2,3},{3,2},{4,5},{5,4},{6,7},{7,6},{8,9},{9,8},{10,11... | collective-permute-start | bytes 6291464 | tf_op jit(solution)/shard_map/ppermute | solution.py:245
  8.1 0.7 collective-permute-start
  8.8 4.2 %collective-permute-start.1 = (bf16[2,64,256]{2,1,0:T(8,128)(2,1)S(1)}, bf16[2,64,256]{2,1,0:T(8,128)(2,1)S(1)}, u32[]{:S(2)}, u32[]{:S(2)}) collective-permute-start(bf16[2,64,256]{2,1,0:T(8,128)(2,1)S(1)} %slice_select_fusion.own0_ref), channel_id=1, source_target_pairs={{17,1},{19,3},{21,5},{23,7},{25,9},{27,11},{29,13},{31,15},{33,17}... | collective-permute-start | bytes 196616 | tf_op jit(solution)/shard_map/ppermute | solution.py:222
  13.0 0.1 convert_reduce_fusion.rank_ref
  13.1 0.1 pad_add_fusion.where_ref
  13.2 0.0 collective-permute-done.2.u1
  13.2 0.0 collective-permute-done.3.v1
  13.2 2.9 %shard_map.78.held_ref = bf16[4,16,256,256]{3,2,1,0:T(8,128)(2,1)S(1)} custom-call(bf16[16,256,256]{2,1,0:T(8,128)(2,1)} %bitcast.13, bf16[16,256,256]{2,1,0:T(8,128)(2,1)} %bitcast.15, bf16[16,256,256]{2,1,0:T(8,128)(2,1)S(1)} %collective-permute-done.2.u1, bf16[16,256,256]{2,1,0:T(8,128)(2,1)} %collective-permute-done.3.v1), custom_call_target="tpu_custom_call" | custom-call | bytes 8388608 | tf_op jit(solution)/shard_map/pallas_call | solution.py:194
  16.2 0.0 collective-permute-done.far0_ref
  16.2 0.0 collective-permute-done.1.next_ref
  16.2 2.7 %shard_map.79 = bf16[4,4,64,256]{3,2,1,0:T(8,128)(2,1)S(1)} custom-call(s32[3]{0:T(128)S(1)} %pad_add_fusion.where_ref, s32[2,16]{1,0:T(2,128)S(1)} %convert_reduce_fusion.rank_ref, bf16[2,64,256]{2,1,0:T(8,128)(2,1)S(1)} %slice_select_fusion.own0_ref, bf16[2,64,256]{2,1,0:T(8,128)(2,1)S(1)} %collective-permute-done.far0_ref, ...), custom_call_target="tpu_custom_call" | custom-call | flops 536870912 | bytes 10485760 | tf_op jit(solution)/shard_map/pallas_call | solution.py:182
  18.9 10.7 %all_to_all.15.got_ref = bf16[4,4,64,256]{3,2,1,0:T(8,128)(2,1)S(1)} all-to-all(bf16[4,4,64,256]{3,2,1,0:T(8,128)(2,1)S(1)} %shard_map.79), channel_id=1, replica_groups={{0,2,4,6},{1,3,5,7},{8,10,12,14},{9,11,13,15},{16,18,20,22},{17,19,21,2..., dimensions={0} | all-to-all | bytes 1048576 | tf_op jit(solution)/shard_map/all_to_all | solution.py:261
  29.6 0.6 shard_map.80
  30.3 15.6 %collective-permute-start.4 = (bf16[2,64,256]{2,1,0:T(8,128)(2,1)S(1)}, bf16[2,64,256]{2,1,0:T(8,128)(2,1)S(1)}, u32[]{:S(2)}, u32[]{:S(2)}) collective-permute-start(bf16[2,64,256]{2,1,0:T(8,128)(2,1)S(1)} %get-tuple-element.14), channel_id=1, source_target_pairs={{0,24},{2,26},{4,28},{6,30},{8,16},{10,18},{12,20},{14,22},{16,40}... | collective-permute-start | bytes 196616 | tf_op jit(solution)/shard_map/ppermute | solution.py:222
  45.8 3.3 %collective-permute-start.5 = (bf16[2,64,256]{2,1,0:T(8,128)(2,1)S(1)}, bf16[2,64,256]{2,1,0:T(8,128)(2,1)S(1)}, u32[]{:S(2)}, u32[]{:S(2)}) collective-permute-start(bf16[2,64,256]{2,1,0:T(8,128)(2,1)S(1)} %get-tuple-element.15), channel_id=1, source_target_pairs={{0,16},{2,18},{4,20},{6,22},{8,24},{10,26},{12,28},{14,30},{16,32}... | collective-permute-start | bytes 196616 | tf_op jit(solution)/shard_map/ppermute | solution.py:222
  49.1 0.0 collective-permute-done.4.far_ref
  49.1 1.7 %collective-permute-done.5.hop_ref = bf16[2,64,256]{2,1,0:T(8,128)(2,1)S(1)} collective-permute-done((bf16[2,64,256]{2,1,0:T(8,128)(2,1)S(1)}, bf16[2,64,256]{2,1,0:T(8,128)(2,1)S(1)}, u32[]{:S(2)}, u32[]{:S(2)}) %collective-permute-start.5) | collective-permute-done | bytes 65568 | tf_op jit(solution)/shard_map/ppermute | solution.py:222
  50.8 2.7 %shard_map.81 = bf16[4,4,64,256]{3,2,1,0:T(8,128)(2,1)S(1)} custom-call(s32[3]{0:T(128)S(1)} %pad_add_fusion.where_ref, s32[2,16]{1,0:T(2,128)S(1)} %convert_reduce_fusion.rank_ref, bf16[2,64,256]{2,1,0:T(8,128)(2,1)S(1)} %collective-permute-done.4.far_ref, bf16[2,64,256]{2,1,0:T(8,128)(2,1)S(1)} %collective-permute-done.5.hop_ref, ...), custom_call_target="tpu_custom_call" | custom-call | flops 536870912 | bytes 10485760 | tf_op jit(solution)/shard_map/pallas_call | solution.py:182
  53.5 9.3 %all_to_all.16.got_ref = bf16[4,4,64,256]{3,2,1,0:T(8,128)(2,1)S(1)} all-to-all(bf16[4,4,64,256]{3,2,1,0:T(8,128)(2,1)S(1)} %shard_map.81), channel_id=1, replica_groups={{0,2,4,6},{1,3,5,7},{8,10,12,14},{9,11,13,15},{16,18,20,22},{17,19,21,2..., dimensions={0} | all-to-all | bytes 1048576 | tf_op jit(solution)/shard_map/all_to_all | solution.py:261
  62.8 0.6 shard_map.82
  63.5 12.8 %collective-permute-start.6 = (bf16[2,64,256]{2,1,0:T(8,128)(2,1)S(1)}, bf16[2,64,256]{2,1,0:T(8,128)(2,1)S(1)}, u32[]{:S(2)}, u32[]{:S(2)}) collective-permute-start(bf16[2,64,256]{2,1,0:T(8,128)(2,1)S(1)} %get-tuple-element.16), channel_id=1, source_target_pairs={{0,24},{2,26},{4,28},{6,30},{8,16},{10,18},{12,20},{14,22},{16,40}... | collective-permute-start | bytes 196616 | tf_op jit(solution)/shard_map/ppermute | solution.py:222
  76.3 1.9 %collective-permute-start.7 = (bf16[2,64,256]{2,1,0:T(8,128)(2,1)S(1)}, bf16[2,64,256]{2,1,0:T(8,128)(2,1)S(1)}, u32[]{:S(2)}, u32[]{:S(2)}) collective-permute-start(bf16[2,64,256]{2,1,0:T(8,128)(2,1)S(1)} %get-tuple-element.17), channel_id=1, source_target_pairs={{0,16},{2,18},{4,20},{6,22},{8,24},{10,26},{12,28},{14,30},{16,32}... | collective-permute-start | bytes 196616 | tf_op jit(solution)/shard_map/ppermute | solution.py:222
  78.2 0.3 collective-permute-done.6.far_ref
  78.5 2.8 %collective-permute-done.7.hop_ref = bf16[2,64,256]{2,1,0:T(8,128)(2,1)S(1)} collective-permute-done((bf16[2,64,256]{2,1,0:T(8,128)(2,1)S(1)}, bf16[2,64,256]{2,1,0:T(8,128)(2,1)S(1)}, u32[]{:S(2)}, u32[]{:S(2)}) %collective-permute-start.7) | collective-permute-done | bytes 65568 | tf_op jit(solution)/shard_map/ppermute | solution.py:222
  81.3 2.7 %shard_map.83 = bf16[4,4,64,256]{3,2,1,0:T(8,128)(2,1)S(1)} custom-call(s32[3]{0:T(128)S(1)} %pad_add_fusion.where_ref, s32[2,16]{1,0:T(2,128)S(1)} %convert_reduce_fusion.rank_ref, bf16[2,64,256]{2,1,0:T(8,128)(2,1)S(1)} %collective-permute-done.6.far_ref, bf16[2,64,256]{2,1,0:T(8,128)(2,1)S(1)} %collective-permute-done.7.hop_ref, ...), custom_call_target="tpu_custom_call" | custom-call | flops 536870912 | bytes 10485760 | tf_op jit(solution)/shard_map/pallas_call | solution.py:182
  84.0 9.6 %all_to_all.17.got_ref = bf16[4,4,64,256]{3,2,1,0:T(8,128)(2,1)S(1)} all-to-all(bf16[4,4,64,256]{3,2,1,0:T(8,128)(2,1)S(1)} %shard_map.83), channel_id=1, replica_groups={{0,2,4,6},{1,3,5,7},{8,10,12,14},{9,11,13,15},{16,18,20,22},{17,19,21,2..., dimensions={0} | all-to-all | bytes 1048576 | tf_op jit(solution)/shard_map/all_to_all | solution.py:261
  93.6 0.6 shard_map.84
  94.3 7.0 %collective-permute-start.8 = (bf16[2,64,256]{2,1,0:T(8,128)(2,1)S(1)}, bf16[2,64,256]{2,1,0:T(8,128)(2,1)S(1)}, u32[]{:S(2)}, u32[]{:S(2)}) collective-permute-start(bf16[2,64,256]{2,1,0:T(8,128)(2,1)S(1)} %get-tuple-element.19), channel_id=1, source_target_pairs={{0,16},{1,9},{2,18},{3,11},{4,20},{5,13},{6,22},{7,15},{8,24},{9,1... | collective-permute-start | bytes 196616 | tf_op jit(solution)/shard_map/ppermute | solution.py:222
  101.3 7.4 %collective-permute-done.8 = bf16[2,64,256]{2,1,0:T(8,128)(2,1)S(1)} collective-permute-done((bf16[2,64,256]{2,1,0:T(8,128)(2,1)S(1)}, bf16[2,64,256]{2,1,0:T(8,128)(2,1)S(1)}, u32[]{:S(2)}, u32[]{:S(2)}) %collective-permute-start.8) | collective-permute-done | bytes 65568 | tf_op jit(solution)/shard_map/ppermute | solution.py:222
  108.8 10.5 %all_gather.11 = bf16[2,64,256]{2,1,0:T(8,128)(2,1)S(1)} all-gather(bf16[1,64,256]{2,1,0:T(8,128)(2,1)S(1)} %constant_dynamic-slice_fusion), channel_id=1, replica_groups={{0,1},{2,3},{4,5},{6,7},{8,9},{10,11},{12,13},{14,15},{16,17},{18,19},{..., dimensions={0}, use_global_device_ids=true | all-gather | bytes 98304 | tf_op jit(solution)/shard_map/all_gather | solution.py:270
  119.3 0.6 broadcast_select_fusion
  (3 shorter events, 0.1 us)
Async XLA Ops:
  3.8 9.4 %collective-permute-start.2 = (bf16[16,256,256]{2,1,0:T(8,128)(2,1)}, bf16[16,256,256]{2,1,0:T(8,128)(2,1)S(1)}, u32[]{:S(2)}, u32[]{:S(2)}) collective-permute-start(bf16[16,256,256]{2,1,0:T(8,128)(2,1)} %bitcast.12), channel_id=1, source_target_pairs={{0,1},{1,0},{2,3},{3,2},{4,5},{5,4},{6,7},{7,6},{8,9},{9,8},{10,11... | collective-permute-start | bytes 6291464 | tf_op jit(solution)/shard_map/ppermute | solution.py:244
  6.0 7.2 %collective-permute-start.3 = (bf16[16,256,256]{2,1,0:T(8,128)(2,1)}, bf16[16,256,256]{2,1,0:T(8,128)(2,1)}, u32[]{:S(2)}, u32[]{:S(2)}) collective-permute-start(bf16[16,256,256]{2,1,0:T(8,128)(2,1)} %bitcast.14), channel_id=1, source_target_pairs={{0,1},{1,0},{2,3},{3,2},{4,5},{5,4},{6,7},{7,6},{8,9},{9,8},{10,11... | collective-permute-start | bytes 6291464 | tf_op jit(solution)/shard_map/ppermute | solution.py:245
  8.1 8.0 %collective-permute-start = (bf16[2,64,256]{2,1,0:T(8,128)(2,1)S(1)}, bf16[2,64,256]{2,1,0:T(8,128)(2,1)S(1)}, u32[]{:S(2)}, u32[]{:S(2)}) collective-permute-start(bf16[2,64,256]{2,1,0:T(8,128)(2,1)S(1)} %slice_select_fusion.own0_ref), channel_id=1, source_target_pairs={{0,8},{2,10},{4,12},{6,14},{8,0},{10,2},{12,4},{14,6},{16,24},{18,... | collective-permute-start | bytes 196616 | tf_op jit(solution)/shard_map/ppermute | solution.py:222
  8.8 7.4 %collective-permute-start.1 = (bf16[2,64,256]{2,1,0:T(8,128)(2,1)S(1)}, bf16[2,64,256]{2,1,0:T(8,128)(2,1)S(1)}, u32[]{:S(2)}, u32[]{:S(2)}) collective-permute-start(bf16[2,64,256]{2,1,0:T(8,128)(2,1)S(1)} %slice_select_fusion.own0_ref), channel_id=1, source_target_pairs={{17,1},{19,3},{21,5},{23,7},{25,9},{27,11},{29,13},{31,15},{33,17}... | collective-permute-start | bytes 196616 | tf_op jit(solution)/shard_map/ppermute | solution.py:222
  30.3 18.9 %collective-permute-start.4 = (bf16[2,64,256]{2,1,0:T(8,128)(2,1)S(1)}, bf16[2,64,256]{2,1,0:T(8,128)(2,1)S(1)}, u32[]{:S(2)}, u32[]{:S(2)}) collective-permute-start(bf16[2,64,256]{2,1,0:T(8,128)(2,1)S(1)} %get-tuple-element.14), channel_id=1, source_target_pairs={{0,24},{2,26},{4,28},{6,30},{8,16},{10,18},{12,20},{14,22},{16,40}... | collective-permute-start | bytes 196616 | tf_op jit(solution)/shard_map/ppermute | solution.py:222
  45.8 5.0 %collective-permute-start.5 = (bf16[2,64,256]{2,1,0:T(8,128)(2,1)S(1)}, bf16[2,64,256]{2,1,0:T(8,128)(2,1)S(1)}, u32[]{:S(2)}, u32[]{:S(2)}) collective-permute-start(bf16[2,64,256]{2,1,0:T(8,128)(2,1)S(1)} %get-tuple-element.15), channel_id=1, source_target_pairs={{0,16},{2,18},{4,20},{6,22},{8,24},{10,26},{12,28},{14,30},{16,32}... | collective-permute-start | bytes 196616 | tf_op jit(solution)/shard_map/ppermute | solution.py:222
  63.5 15.1 %collective-permute-start.6 = (bf16[2,64,256]{2,1,0:T(8,128)(2,1)S(1)}, bf16[2,64,256]{2,1,0:T(8,128)(2,1)S(1)}, u32[]{:S(2)}, u32[]{:S(2)}) collective-permute-start(bf16[2,64,256]{2,1,0:T(8,128)(2,1)S(1)} %get-tuple-element.16), channel_id=1, source_target_pairs={{0,24},{2,26},{4,28},{6,30},{8,16},{10,18},{12,20},{14,22},{16,40}... | collective-permute-start | bytes 196616 | tf_op jit(solution)/shard_map/ppermute | solution.py:222
  76.3 5.0 %collective-permute-start.7 = (bf16[2,64,256]{2,1,0:T(8,128)(2,1)S(1)}, bf16[2,64,256]{2,1,0:T(8,128)(2,1)S(1)}, u32[]{:S(2)}, u32[]{:S(2)}) collective-permute-start(bf16[2,64,256]{2,1,0:T(8,128)(2,1)S(1)} %get-tuple-element.17), channel_id=1, source_target_pairs={{0,16},{2,18},{4,20},{6,22},{8,24},{10,26},{12,28},{14,30},{16,32}... | collective-permute-start | bytes 196616 | tf_op jit(solution)/shard_map/ppermute | solution.py:222
  94.3 14.4 %collective-permute-start.8 = (bf16[2,64,256]{2,1,0:T(8,128)(2,1)S(1)}, bf16[2,64,256]{2,1,0:T(8,128)(2,1)S(1)}, u32[]{:S(2)}, u32[]{:S(2)}) collective-permute-start(bf16[2,64,256]{2,1,0:T(8,128)(2,1)S(1)} %get-tuple-element.19), channel_id=1, source_target_pairs={{0,16},{1,9},{2,18},{3,11},{4,20},{5,13},{6,22},{7,15},{8,24},{9,1... | collective-permute-start | bytes 196616 | tf_op jit(solution)/shard_map/ppermute | solution.py:222

commit v4 on v3

--- a/solution.py
+++ b/solution.py
@@ -27,11 +27,16 @@
     return lax.dot_general(a, b, (((1,), (0,)), ((), ())), preferred_element_type=F32)
 
 
+def my_place():
+    place = lax.axis_index("xy")
+    return lax.rem(place, 2), lax.div(place, 8)
+
+
 def coefficients(product, limit):
     rank = product.shape[1] // 2
     real = product[:HALF, :rank] - product[HALF:, rank:]
     imag = product[:HALF, rank:] + product[HALF:, :rank]
-    keep = lax.broadcasted_iota(jnp.int32, real.shape, 1) < limit
+    keep = lax.broadcasted_iota(jnp.int32, real.shape, 1) < jnp.broadcast_to(limit, real.shape)
     real = jnp.where(keep, real, 0.0).astype(BF)
     imag = jnp.where(keep, imag, 0.0).astype(BF)
     top = jnp.concatenate([real, -imag], axis=1)
@@ -62,9 +67,8 @@
     return total.astype(BF)
 
 
-def spread(where_ref, rank_ref, own, far, down, held_ref, out_ref):
-    core = where_ref[0]
-    z_own = where_ref[1]
+def spread(rank_ref, own, far, down, held_ref, out_ref):
+    core, z_own = my_place()
 
     @pl.when(core == 0)
     def _():
@@ -86,7 +90,7 @@
                     j = g * SIZE + k
                     for n in range(PAIR):
                         product = dot_rows(traces[1 - n], held_ref[2 * n, j])
-                        coefs[n, j] = coefficients(product, rank_ref[1 - n, j])
+                        coefs[n, j] = coefficients(product, rank_ref[pl.ds((1 - n) * 16 + j, 1), :])
                 if g > 0:
                     j = (g - 1) * SIZE + k
                     total = dot_cols(coefs[0, j], held_ref[1, j]) + dot_cols(coefs[1, j], held_ref[3, j])
@@ -94,33 +98,30 @@
                     out_ref[x, slot] = total.astype(BF)
 
 
-def first_spread_kernel(where_ref, rank_ref, own0_ref, far0_ref, next_ref, held_ref, out_ref):
+def first_spread_kernel(rank_ref, own0_ref, first_ref, held_ref, out_ref):
     spread(
-        where_ref,
         rank_ref,
         lambda c: own0_ref[c],
-        lambda c: far0_ref[c],
-        lambda c: next_ref[c],
+        lambda c: first_ref[c],
+        lambda c: first_ref[c],
         held_ref,
         out_ref,
     )
 
 
-def spread_kernel(where_ref, rank_ref, far_ref, hop_ref, own0_ref, far0_ref, next_ref, held_ref, out_ref):
+def spread_kernel(rank_ref, far_ref, hop_ref, own0_ref, first_ref, held_ref, out_ref):
     spread(
-        where_ref,
         rank_ref,
         lambda c: added(own0_ref[c], hop_ref[c]),
-        lambda c: added(far0_ref[c], far_ref[c]),
-        lambda c: added(next_ref[c], hop_ref[c], far_ref[c]),
+        lambda c: added(first_ref[c], far_ref[c]),
+        lambda c: added(first_ref[c], hop_ref[c], far_ref[c]),
         held_ref,
         out_ref,
     )
 
 
-def gather_kernel(where_ref, rank_ref, got_ref, held_ref, far_ref, hop_ref):
-    core = where_ref[0]
-    z_own = where_ref[1]
+def gather_kernel(rank_ref, got_ref, held_ref, far_ref, hop_ref):
+    core, z_own = my_place()
 
     @pl.when(core == 0)
     def _():
@@ -133,7 +134,7 @@
                         j = g * SIZE + k
                         x, slot = place_of(j)
                         product = dot_rows(got_ref[x, slot], held_ref[2 * row + 1, j])
-                        coefs[row, j] = coefficients(product, rank_ref[row, j])
+                        coefs[row, j] = coefficients(product, rank_ref[pl.ds(row * 16 + j, 1), :])
                     if g > 0:
                         j = (g - 1) * SIZE + k
                         part = dot_cols(coefs[row, j], held_ref[2 * row, j])
@@ -175,18 +176,17 @@
     packed_ref[pl.ds(2 * ROWS, 16), :] = ranks.astype(F32).astype(BF)
 
 
-def call(kernel, outs, scalars, arrays):
-    smem = pl.BlockSpec(memory_space=pltpu.SMEM)
+def call(kernel, outs, arrays):
     vmem = pl.BlockSpec(memory_space=pltpu.VMEM)
     arrays = [pltpu.with_memory_space_constraint(a, pltpu.VMEM) for a in arrays]
     return pl.pallas_call(
         kernel,
         out_shape=outs,
-        in_specs=[smem] * len(scalars) + [vmem] * len(arrays),
+        in_specs=[vmem] * len(arrays),
         out_specs=jax.tree.map(lambda _: vmem, outs),
         compiler_params=pltpu.CompilerParams(vmem_limit_bytes=LIMIT),
         cost_estimate=pl.CostEstimate(flops=64 * 2 * 64 * 256 * 256, bytes_accessed=10 * 1024 * 1024, transcendentals=0),
-    )(*scalars, *arrays)
+    )(*arrays)
 
 
 def load(own, others):
@@ -206,7 +206,6 @@
     layer = lax.axis_index("gz")
     place = lax.axis_index("xy")
     core = place % 2
-    z_own = place // 8
     both = ("gz", "xy")
     width = u_factor.shape[-1]
     max_rank = u_factor.shape[-2]
@@ -244,22 +243,19 @@
     u_other = lax.ppermute(u_sent, "xy", [(i, i ^ 1) for i in range(16)])
     v_other = lax.ppermute(v_sent, "xy", [(i, i ^ 1) for i in range(16)])
     mine = jnp.where(core == 0, chip[:, :ROWS], chip[:, ROWS : 2 * ROWS])
-    limits = (chip[:, 2 * ROWS :, 0].astype(F32) * step).astype(jnp.int32)
-    far0 = send(mine, lambda l, i: (l, i ^ 8) if i % 2 == 0 else None)
-    following = send(mine, lambda l, i: (l - 1, i) if i % 2 == 1 else None)
-    where = jnp.stack([core, z_own, layer]).astype(jnp.int32)
-    scalars = (where, limits)
+    limits = (chip[:, 2 * ROWS :, :max_rank].astype(F32) * step).astype(jnp.int32).reshape(PAIR * 16, max_rank)
+    first = send(mine, lambda l, i: (l, i ^ 8) if i % 2 == 0 else (l - 1, i))
     held = load((u_own, v_own), (u_other, v_other))
     pair_shape = jax.ShapeDtypeStruct((PAIR, ROWS, width), BF)
     ring_shape = jax.ShapeDtypeStruct((XS, 2 * PAIR, ROWS, width), BF)
 
     for sweep in range(STEPS):
         if sweep == 0:
-            sent = call(first_spread_kernel, ring_shape, scalars, (mine, far0, following, held))
+            sent = call(first_spread_kernel, ring_shape, (limits, mine, first, held))
         else:
-            sent = call(spread_kernel, ring_shape, scalars, (far, hop, mine, far0, following, held))
+            sent = call(spread_kernel, ring_shape, (limits, far, hop, mine, first, held))
         got = lax.all_to_all(sent, "xy", 0, 0, axis_index_groups=rings)
-        away, near = call(gather_kernel, (pair_shape, pair_shape), scalars, (got, held))
+        away, near = call(gather_kernel, (pair_shape, pair_shape), (limits, got, held))
         if sweep < STEPS - 1:
             far = send(away, ahead_far)
             hop = send(near, ahead)

time: 120 us -> 117 us (0.975)
  Pallas kernels: 13.7 us -> 10.3 us
  starting transfers between devices: 49.7 us -> 48.5 us
    pallas_call x6, Pallas kernels: 9.88 us -> 6.52 us  [call(): pl.pallas_call(kernel, out_shape=outs, in_specs=[vmem] * len(arrays), out...]
    ppermute x7 -> x6, starting transfers between devices: 45.4 us -> 44.2 us  [send(): return lax.ppermute(block, both, route)]
    ppermute x7 -> x6, waiting for transfers between devices: 12.2 us -> 12.5 us  [send(): return lax.ppermute(block, both, route)]
  transfers between devices with their start and end apart: 9 -> 8, of which waited for: 4 -> 6; matrix products, arithmetic and copies ran while one was open for 0% -> 0% of each run, Pallas kernels for 2% -> 3%
where the time goes in v4:
time: 117 us
  starting transfers between devices  48.5 us (41%)
  blocking collectives  42.9 us (37%)
  waiting for transfers between devices  13.3 us (11%)
  Pallas kernels  10.3 us (9%)
    ppermute x6, starting transfers between devices, send(): return lax.ppermute(block, both, route)  44.2 us
    all_to_all x3, blocking collectives, on_device(): got = lax.all_to_all(sent, 'xy', 0, 0, axis_index_groups=rings)  29.7 us
    ppermute x6, waiting for transfers between devices, send(): return lax.ppermute(block, both, route)  12.5 us
    all_gather x1, blocking collectives, on_device(): lax.all_gather(final[1 - core], 'xy', axis=0, axis_index_groups=pairs)  11 us
    pallas_call x6, Pallas kernels, call(): pl.pallas_call(kernel, out_shape=outs, in_specs=[vmem] * len(arrays), out...  6.52 us
    pallas_call x1, Pallas kernels, load(): pl.pallas_call(load_kernel, out_shape=pltpu.VMEM((4,) + own[0].shape, BF)...  2.93 us
  transfers between devices with their start and end apart: 8, of which 6 were waited for; matrix products, arithmetic and copies ran while one was open for 0% of the time, Pallas kernels for 3%

profile of v4, /device:TPU:65, one launch (start us, length us, event | category | flops | bytes accessed | tf_op | source)
XLA Modules:
  0.0 116.6 jit_solution(5531557676622275568)
XLA Ops:
  0.6 0.9 shard_map.77
  1.5 2.2 %all-gather = bf16[288,256]{1,0:T(8,128)(2,1)S(1)} all-gather(bf16[144,256]{1,0:T(8,128)(2,1)S(1)} %shard_map.77), channel_id=2, replica_groups={{0,1},{2,3},{4,5},{6,7},{8,9},{10,11},{12,13},{14,15},{16,17},{18,19},{..., dimensions={0}, use_global_device_ids=true | all-gather | bytes 221184 | tf_op jit(solution)/shard_map/all_gather | solution.py:239
  3.8 2.3 %collective-permute-start.1 = (bf16[16,256,256]{2,1,0:T(8,128)(2,1)}, bf16[16,256,256]{2,1,0:T(8,128)(2,1)S(1)}, u32[]{:S(2)}, u32[]{:S(2)}) collective-permute-start(bf16[16,256,256]{2,1,0:T(8,128)(2,1)} %bitcast.17), channel_id=1, source_target_pairs={{0,1},{1,0},{2,3},{3,2},{4,5},{5,4},{6,7},{7,6},{8,9},{9,8},{10,11... | collective-permute-start | bytes 6291464 | tf_op jit(solution)/shard_map/ppermute | solution.py:243
  6.0 2.1 %collective-permute-start.2 = (bf16[16,256,256]{2,1,0:T(8,128)(2,1)}, bf16[16,256,256]{2,1,0:T(8,128)(2,1)}, u32[]{:S(2)}, u32[]{:S(2)}) collective-permute-start(bf16[16,256,256]{2,1,0:T(8,128)(2,1)} %bitcast.19), channel_id=1, source_target_pairs={{0,1},{1,0},{2,3},{3,2},{4,5},{5,4},{6,7},{7,6},{8,9},{9,8},{10,11... | collective-permute-start | bytes 6291464 | tf_op jit(solution)/shard_map/ppermute | solution.py:244
  8.1 4.2 %collective-permute-start = (bf16[2,64,256]{2,1,0:T(8,128)(2,1)S(1)}, bf16[2,64,256]{2,1,0:T(8,128)(2,1)S(1)}, u32[]{:S(2)}, u32[]{:S(2)}) collective-permute-start(bf16[2,64,256]{2,1,0:T(8,128)(2,1)S(1)} %slice_select_fusion.own0_ref), channel_id=1, source_target_pairs={{0,8},{2,10},{4,12},{6,14},{8,0},{10,2},{12,4},{14,6},{16,24},{17,... | collective-permute-start | bytes 196616 | tf_op jit(solution)/shard_map/ppermute | solution.py:221
  12.4 0.0 collective-permute-done.1.u1
  12.4 0.8 collective-permute-done.2.v1
  13.2 2.9 %shard_map.78.held_ref = bf16[4,16,256,256]{3,2,1,0:T(8,128)(2,1)S(1)} custom-call(bf16[16,256,256]{2,1,0:T(8,128)(2,1)} %bitcast.18, bf16[16,256,256]{2,1,0:T(8,128)(2,1)} %bitcast.20, bf16[16,256,256]{2,1,0:T(8,128)(2,1)S(1)} %collective-permute-done.1.u1, bf16[16,256,256]{2,1,0:T(8,128)(2,1)} %collective-permute-done.2.v1), custom_call_target="tpu_custom_call" | custom-call | bytes 8388608 | tf_op jit(solution)/shard_map/pallas_call | solution.py:194
  16.1 0.0 collective-permute-done.first_ref
  16.1 2.1 %shard_map.79 = bf16[4,4,64,256]{3,2,1,0:T(8,128)(2,1)S(1)} custom-call(s32[32,128]{1,0:T(8,128)S(1)} %bitcast.11, bf16[2,64,256]{2,1,0:T(8,128)(2,1)S(1)} %slice_select_fusion.own0_ref, bf16[2,64,256]{2,1,0:T(8,128)(2,1)S(1)} %collective-permute-done.first_ref, bf16[4,16,256,256]{3,2,1,0:T(8,128)(2,1)S(1)} %shard_map.78.held_ref), custom_call_target="tpu_custom_call" | custom-call | flops 536870912 | bytes 10485760 | tf_op jit(solution)/shard_map/pallas_call | solution.py:182
  18.2 10.7 %all_to_all.15.got_ref = bf16[4,4,64,256]{3,2,1,0:T(8,128)(2,1)S(1)} all-to-all(bf16[4,4,64,256]{3,2,1,0:T(8,128)(2,1)S(1)} %shard_map.79), channel_id=1, replica_groups={{0,2,4,6},{1,3,5,7},{8,10,12,14},{9,11,13,15},{16,18,20,22},{17,19,21,2..., dimensions={0} | all-to-all | bytes 1048576 | tf_op jit(solution)/shard_map/all_to_all | solution.py:257
  29.0 0.1 shard_map.80
  29.1 15.6 %collective-permute-start.3 = (bf16[2,64,256]{2,1,0:T(8,128)(2,1)S(1)}, bf16[2,64,256]{2,1,0:T(8,128)(2,1)S(1)}, u32[]{:S(2)}, u32[]{:S(2)}) collective-permute-start(bf16[2,64,256]{2,1,0:T(8,128)(2,1)S(1)} %get-tuple-element.14), channel_id=1, source_target_pairs={{0,24},{2,26},{4,28},{6,30},{8,16},{10,18},{12,20},{14,22},{16,40}... | collective-permute-start | bytes 196616 | tf_op jit(solution)/shard_map/ppermute | solution.py:221
  44.7 3.3 %collective-permute-start.4 = (bf16[2,64,256]{2,1,0:T(8,128)(2,1)S(1)}, bf16[2,64,256]{2,1,0:T(8,128)(2,1)S(1)}, u32[]{:S(2)}, u32[]{:S(2)}) collective-permute-start(bf16[2,64,256]{2,1,0:T(8,128)(2,1)S(1)} %get-tuple-element.15), channel_id=1, source_target_pairs={{0,16},{2,18},{4,20},{6,22},{8,24},{10,26},{12,28},{14,30},{16,32}... | collective-permute-start | bytes 196616 | tf_op jit(solution)/shard_map/ppermute | solution.py:221
  48.0 0.7 collective-permute-done.3.far_ref
  48.7 1.0 collective-permute-done.4.hop_ref
  49.7 2.1 %shard_map.81 = bf16[4,4,64,256]{3,2,1,0:T(8,128)(2,1)S(1)} custom-call(s32[32,128]{1,0:T(8,128)S(1)} %bitcast.13, bf16[2,64,256]{2,1,0:T(8,128)(2,1)S(1)} %collective-permute-done.3.far_ref, bf16[2,64,256]{2,1,0:T(8,128)(2,1)S(1)} %collective-permute-done.4.hop_ref, bf16[2,64,256]{2,1,0:T(8,128)(2,1)S(1)} %slice_select_fusion.own0_ref, ...), custom_call_target="tpu_custom_call" | custom-call | flops 536870912 | bytes 10485760 | tf_op jit(solution)/shard_map/pallas_call | solution.py:182
  51.8 9.3 %all_to_all.16.got_ref = bf16[4,4,64,256]{3,2,1,0:T(8,128)(2,1)S(1)} all-to-all(bf16[4,4,64,256]{3,2,1,0:T(8,128)(2,1)S(1)} %shard_map.81), channel_id=1, replica_groups={{0,2,4,6},{1,3,5,7},{8,10,12,14},{9,11,13,15},{16,18,20,22},{17,19,21,2..., dimensions={0} | all-to-all | bytes 1048576 | tf_op jit(solution)/shard_map/all_to_all | solution.py:257
  61.1 0.1 shard_map.82
  61.2 12.7 %collective-permute-start.5 = (bf16[2,64,256]{2,1,0:T(8,128)(2,1)S(1)}, bf16[2,64,256]{2,1,0:T(8,128)(2,1)S(1)}, u32[]{:S(2)}, u32[]{:S(2)}) collective-permute-start(bf16[2,64,256]{2,1,0:T(8,128)(2,1)S(1)} %get-tuple-element.16), channel_id=1, source_target_pairs={{0,24},{2,26},{4,28},{6,30},{8,16},{10,18},{12,20},{14,22},{16,40}... | collective-permute-start | bytes 196616 | tf_op jit(solution)/shard_map/ppermute | solution.py:221
  73.9 1.9 %collective-permute-start.6 = (bf16[2,64,256]{2,1,0:T(8,128)(2,1)S(1)}, bf16[2,64,256]{2,1,0:T(8,128)(2,1)S(1)}, u32[]{:S(2)}, u32[]{:S(2)}) collective-permute-start(bf16[2,64,256]{2,1,0:T(8,128)(2,1)S(1)} %get-tuple-element.17), channel_id=1, source_target_pairs={{0,16},{2,18},{4,20},{6,22},{8,24},{10,26},{12,28},{14,30},{16,32}... | collective-permute-start | bytes 196616 | tf_op jit(solution)/shard_map/ppermute | solution.py:221
  75.9 0.4 collective-permute-done.5.far_ref
  76.3 2.7 %collective-permute-done.6.hop_ref = bf16[2,64,256]{2,1,0:T(8,128)(2,1)S(1)} collective-permute-done((bf16[2,64,256]{2,1,0:T(8,128)(2,1)S(1)}, bf16[2,64,256]{2,1,0:T(8,128)(2,1)S(1)}, u32[]{:S(2)}, u32[]{:S(2)}) %collective-permute-start.6) | collective-permute-done | bytes 65568 | tf_op jit(solution)/shard_map/ppermute | solution.py:221
  79.0 2.1 %shard_map.83 = bf16[4,4,64,256]{3,2,1,0:T(8,128)(2,1)S(1)} custom-call(s32[32,128]{1,0:T(8,128)S(1)} %bitcast.15, bf16[2,64,256]{2,1,0:T(8,128)(2,1)S(1)} %collective-permute-done.5.far_ref, bf16[2,64,256]{2,1,0:T(8,128)(2,1)S(1)} %collective-permute-done.6.hop_ref, bf16[2,64,256]{2,1,0:T(8,128)(2,1)S(1)} %slice_select_fusion.own0_ref, ...), custom_call_target="tpu_custom_call" | custom-call | flops 536870912 | bytes 10485760 | tf_op jit(solution)/shard_map/pallas_call | solution.py:182
  81.1 9.6 %all_to_all.17.got_ref = bf16[4,4,64,256]{3,2,1,0:T(8,128)(2,1)S(1)} all-to-all(bf16[4,4,64,256]{3,2,1,0:T(8,128)(2,1)S(1)} %shard_map.83), channel_id=1, replica_groups={{0,2,4,6},{1,3,5,7},{8,10,12,14},{9,11,13,15},{16,18,20,22},{17,19,21,2..., dimensions={0} | all-to-all | bytes 1048576 | tf_op jit(solution)/shard_map/all_to_all | solution.py:257
  90.7 0.1 shard_map.84
  90.8 6.5 %collective-permute-start.7 = (bf16[2,64,256]{2,1,0:T(8,128)(2,1)S(1)}, bf16[2,64,256]{2,1,0:T(8,128)(2,1)S(1)}, u32[]{:S(2)}, u32[]{:S(2)}) collective-permute-start(bf16[2,64,256]{2,1,0:T(8,128)(2,1)S(1)} %get-tuple-element.19), channel_id=1, source_target_pairs={{0,16},{1,9},{2,18},{3,11},{4,20},{5,13},{6,22},{7,15},{8,24},{9,1... | collective-permute-start | bytes 196616 | tf_op jit(solution)/shard_map/ppermute | solution.py:221
  97.2 7.6 %collective-permute-done.7 = bf16[2,64,256]{2,1,0:T(8,128)(2,1)S(1)} collective-permute-done((bf16[2,64,256]{2,1,0:T(8,128)(2,1)S(1)}, bf16[2,64,256]{2,1,0:T(8,128)(2,1)S(1)}, u32[]{:S(2)}, u32[]{:S(2)}) %collective-permute-start.7) | collective-permute-done | bytes 65568 | tf_op jit(solution)/shard_map/ppermute | solution.py:221
  104.9 11.0 %all_gather.11 = bf16[2,64,256]{2,1,0:T(8,128)(2,1)S(1)} all-gather(bf16[1,64,256]{2,1,0:T(8,128)(2,1)S(1)} %constant_dynamic-slice_fusion), channel_id=1, replica_groups={{0,1},{2,3},{4,5},{6,7},{8,9},{10,11},{12,13},{14,15},{16,17},{18,19},{..., dimensions={0}, use_global_device_ids=true | all-gather | bytes 98304 | tf_op jit(solution)/shard_map/all_gather | solution.py:266
  115.9 0.6 broadcast_select_fusion
  (4 shorter events, 0.1 us)
Async XLA Ops:
  3.8 8.6 %collective-permute-start.1 = (bf16[16,256,256]{2,1,0:T(8,128)(2,1)}, bf16[16,256,256]{2,1,0:T(8,128)(2,1)S(1)}, u32[]{:S(2)}, u32[]{:S(2)}) collective-permute-start(bf16[16,256,256]{2,1,0:T(8,128)(2,1)} %bitcast.17), channel_id=1, source_target_pairs={{0,1},{1,0},{2,3},{3,2},{4,5},{5,4},{6,7},{7,6},{8,9},{9,8},{10,11... | collective-permute-start | bytes 6291464 | tf_op jit(solution)/shard_map/ppermute | solution.py:243
  6.0 7.1 %collective-permute-start.2 = (bf16[16,256,256]{2,1,0:T(8,128)(2,1)}, bf16[16,256,256]{2,1,0:T(8,128)(2,1)}, u32[]{:S(2)}, u32[]{:S(2)}) collective-permute-start(bf16[16,256,256]{2,1,0:T(8,128)(2,1)} %bitcast.19), channel_id=1, source_target_pairs={{0,1},{1,0},{2,3},{3,2},{4,5},{5,4},{6,7},{7,6},{8,9},{9,8},{10,11... | collective-permute-start | bytes 6291464 | tf_op jit(solution)/shard_map/ppermute | solution.py:244
  8.1 8.0 %collective-permute-start = (bf16[2,64,256]{2,1,0:T(8,128)(2,1)S(1)}, bf16[2,64,256]{2,1,0:T(8,128)(2,1)S(1)}, u32[]{:S(2)}, u32[]{:S(2)}) collective-permute-start(bf16[2,64,256]{2,1,0:T(8,128)(2,1)S(1)} %slice_select_fusion.own0_ref), channel_id=1, source_target_pairs={{0,8},{2,10},{4,12},{6,14},{8,0},{10,2},{12,4},{14,6},{16,24},{17,... | collective-permute-start | bytes 196616 | tf_op jit(solution)/shard_map/ppermute | solution.py:221
  29.1 19.6 %collective-permute-start.3 = (bf16[2,64,256]{2,1,0:T(8,128)(2,1)S(1)}, bf16[2,64,256]{2,1,0:T(8,128)(2,1)S(1)}, u32[]{:S(2)}, u32[]{:S(2)}) collective-permute-start(bf16[2,64,256]{2,1,0:T(8,128)(2,1)S(1)} %get-tuple-element.14), channel_id=1, source_target_pairs={{0,24},{2,26},{4,28},{6,30},{8,16},{10,18},{12,20},{14,22},{16,40}... | collective-permute-start | bytes 196616 | tf_op jit(solution)/shard_map/ppermute | solution.py:221
  44.7 5.0 %collective-permute-start.4 = (bf16[2,64,256]{2,1,0:T(8,128)(2,1)S(1)}, bf16[2,64,256]{2,1,0:T(8,128)(2,1)S(1)}, u32[]{:S(2)}, u32[]{:S(2)}) collective-permute-start(bf16[2,64,256]{2,1,0:T(8,128)(2,1)S(1)} %get-tuple-element.15), channel_id=1, source_target_pairs={{0,16},{2,18},{4,20},{6,22},{8,24},{10,26},{12,28},{14,30},{16,32}... | collective-permute-start | bytes 196616 | tf_op jit(solution)/shard_map/ppermute | solution.py:221
  61.2 15.0 %collective-permute-start.5 = (bf16[2,64,256]{2,1,0:T(8,128)(2,1)S(1)}, bf16[2,64,256]{2,1,0:T(8,128)(2,1)S(1)}, u32[]{:S(2)}, u32[]{:S(2)}) collective-permute-start(bf16[2,64,256]{2,1,0:T(8,128)(2,1)S(1)} %get-tuple-element.16), channel_id=1, source_target_pairs={{0,24},{2,26},{4,28},{6,30},{8,16},{10,18},{12,20},{14,22},{16,40}... | collective-permute-start | bytes 196616 | tf_op jit(solution)/shard_map/ppermute | solution.py:221
  73.9 5.0 %collective-permute-start.6 = (bf16[2,64,256]{2,1,0:T(8,128)(2,1)S(1)}, bf16[2,64,256]{2,1,0:T(8,128)(2,1)S(1)}, u32[]{:S(2)}, u32[]{:S(2)}) collective-permute-start(bf16[2,64,256]{2,1,0:T(8,128)(2,1)S(1)} %get-tuple-element.17), channel_id=1, source_target_pairs={{0,16},{2,18},{4,20},{6,22},{8,24},{10,26},{12,28},{14,30},{16,32}... | collective-permute-start | bytes 196616 | tf_op jit(solution)/shard_map/ppermute | solution.py:221
  90.8 14.1 %collective-permute-start.7 = (bf16[2,64,256]{2,1,0:T(8,128)(2,1)S(1)}, bf16[2,64,256]{2,1,0:T(8,128)(2,1)S(1)}, u32[]{:S(2)}, u32[]{:S(2)}) collective-permute-start(bf16[2,64,256]{2,1,0:T(8,128)(2,1)S(1)} %get-tuple-element.19), channel_id=1, source_target_pairs={{0,16},{1,9},{2,18},{3,11},{4,20},{5,13},{6,22},{7,15},{8,24},{9,1... | collective-permute-start | bytes 196616 | tf_op jit(solution)/shard_map/ppermute | solution.py:221

commit v5 on v4

--- a/solution.py
+++ b/solution.py
@@ -29,7 +29,8 @@
 
 def my_place():
     place = lax.axis_index("xy")
-    return lax.rem(place, 2), lax.div(place, 8)
+    z_own = lax.div(place, 8)
+    return lax.rem(place + z_own, 2), z_own
 
 
 def coefficients(product, limit):
@@ -48,8 +49,13 @@
     return z * 8 + x * 2 + c
 
 
-def load_kernel(u0, v0, u1, v1, held_ref, sems):
-    copies = [pltpu.make_async_copy(ref, held_ref.at[n], sems.at[n]) for n, ref in enumerate((u0, v0, u1, v1))]
+def load_kernel(u_own, v_own, u_other, v_other, held_ref, sems):
+    own = 2 * lax.rem(lax.axis_index("xy"), 2)
+    other = 2 - own
+    copies = [
+        pltpu.make_async_copy(ref, held_ref.at[slot], sems.at[n])
+        for n, (ref, slot) in enumerate(((u_own, own), (v_own, own + 1), (u_other, other), (v_other, other + 1)))
+    ]
     for copy in copies:
         copy.start()
     for copy in copies:
@@ -68,9 +74,9 @@
 
 
 def spread(rank_ref, own, far, down, held_ref, out_ref):
-    core, z_own = my_place()
-
-    @pl.when(core == 0)
+    role, z_own = my_place()
+
+    @pl.when(role == 0)
     def _():
         for c in range(PAIR):
             near_block = own(c)
@@ -80,7 +86,7 @@
                 for x in range(XS):
                     out_ref[x, z * PAIR + c] = block
 
-    @pl.when(core == 1)
+    @pl.when(role == 1)
     def _():
         traces = [down(c) for c in range(PAIR)]
         coefs = {}
@@ -89,8 +95,8 @@
                 if g < GROUPS:
                     j = g * SIZE + k
                     for n in range(PAIR):
-                        product = dot_rows(traces[1 - n], held_ref[2 * n, j])
-                        coefs[n, j] = coefficients(product, rank_ref[pl.ds((1 - n) * 16 + j, 1), :])
+                        product = dot_rows(traces[n], held_ref[2 * n, j])
+                        coefs[n, j] = coefficients(product, rank_ref[pl.ds(n * 16 + j, 1), :])
                 if g > 0:
                     j = (g - 1) * SIZE + k
                     total = dot_cols(coefs[0, j], held_ref[1, j]) + dot_cols(coefs[1, j], held_ref[3, j])
@@ -121,9 +127,9 @@
 
 
 def gather_kernel(rank_ref, got_ref, held_ref, far_ref, hop_ref):
-    core, z_own = my_place()
-
-    @pl.when(core == 0)
+    role, z_own = my_place()
+
+    @pl.when(role == 0)
     def _():
         totals = [None, None]
         coefs = {}
@@ -144,7 +150,7 @@
             hop_ref[row] = block
             far_ref[row] = block
 
-    @pl.when(core == 1)
+    @pl.when(role == 1)
     def _():
         for c in range(PAIR):
             sums = []
@@ -206,6 +212,7 @@
     layer = lax.axis_index("gz")
     place = lax.axis_index("xy")
     core = place % 2
+    up_here = (place + place // 8) % 2 == 0
     both = ("gz", "xy")
     width = u_factor.shape[-1]
     max_rank = u_factor.shape[-2]
@@ -220,11 +227,17 @@
                     route.append((l * 16 + i, to[0] * 16 + to[1]))
         return lax.ppermute(block, both, route)
 
+    def is_up(i):
+        return (i + i // 8) % 2 == 0
+
+    def far_of(l, i):
+        return l, i ^ 9
+
     def ahead(l, i):
-        return (l + 1, i) if i % 2 == 0 else (l - 1, i)
+        return (l + 1, i) if is_up(i) else (l - 1, i)
 
     def ahead_far(l, i):
-        return (l + 1, i ^ 8) if i % 2 == 0 else (l - 1, i ^ 8)
+        return far_of(*ahead(l, i))
 
     pairs = [[2 * k, 2 * k + 1] for k in range(8)]
     rings = [[block_of(x, z, c) for x in range(XS)] for z in range(2) for c in range(2)]
@@ -242,9 +255,9 @@
     u_sent, v_sent, chip = lax.optimization_barrier((u_own, v_own, chip))
     u_other = lax.ppermute(u_sent, "xy", [(i, i ^ 1) for i in range(16)])
     v_other = lax.ppermute(v_sent, "xy", [(i, i ^ 1) for i in range(16)])
-    mine = jnp.where(core == 0, chip[:, :ROWS], chip[:, ROWS : 2 * ROWS])
+    mine = jnp.where(up_here, chip[:, :ROWS], chip[:, ROWS : 2 * ROWS])
     limits = (chip[:, 2 * ROWS :, :max_rank].astype(F32) * step).astype(jnp.int32).reshape(PAIR * 16, max_rank)
-    first = send(mine, lambda l, i: (l, i ^ 8) if i % 2 == 0 else (l - 1, i))
+    first = send(mine, lambda l, i: far_of(l, i) if is_up(i) else ahead(l, i))
     held = load((u_own, v_own), (u_other, v_other))
     pair_shape = jax.ShapeDtypeStruct((PAIR, ROWS, width), BF)
     ring_shape = jax.ShapeDtypeStruct((XS, 2 * PAIR, ROWS, width), BF)
@@ -254,20 +267,21 @@
             sent = call(first_spread_kernel, ring_shape, (limits, mine, first, held))
         else:
             sent = call(spread_kernel, ring_shape, (limits, far, hop, mine, first, held))
-        got = lax.all_to_all(sent, "xy", 0, 0, axis_index_groups=rings)
+        got = lax.all_to_all(sent.reshape(XS * 2 * PAIR * ROWS, width), "xy", 0, 0, axis_index_groups=rings, tiled=True)
+        got = got.reshape(sent.shape)
         away, near = call(gather_kernel, (pair_shape, pair_shape), (limits, got, held))
         if sweep < STEPS - 1:
             far = send(away, ahead_far)
             hop = send(near, ahead)
 
-    last = send(away, lambda l, i: (l + 1, i) if i % 2 == 0 else (l, i ^ 8))
-    kept_sum = jnp.where(core == 0, jnp.zeros_like(near), near)
+    last = send(away, lambda l, i: ahead(l, i) if is_up(i) else far_of(l, i))
+    kept_sum = jnp.where(up_here, jnp.zeros_like(near), near)
     final = (mine.astype(F32) + (kept_sum.astype(F32) + last.astype(F32))).astype(BF)
     swapped = lax.all_gather(final[1 - core], "xy", axis=0, axis_index_groups=pairs)
     kept = final[core]
     other = swapped[1 - core]
-    up_trace = jnp.where(core == 0, kept, other).reshape(up_source.shape)
-    down_trace = jnp.where(core == 0, other, kept).reshape(up_source.shape)
+    up_trace = jnp.where(up_here, kept, other).reshape(up_source.shape)
+    down_trace = jnp.where(up_here, other, kept).reshape(up_source.shape)
     return up_trace, down_trace
 
 

time: 117 us -> 117 us (level)
  the two profiles are of different devices: /device:TPU:65 before, /device:TPU:57 now
where the time goes in v5:
time: 117 us; the launch traced here: 116 us
  starting transfers between devices  45.9 us (39%)
  blocking collectives  36 us (31%)
  waiting for transfers between devices  22.4 us (19%)
  Pallas kernels  10.3 us (9%)
    ppermute x6, starting transfers between devices, send(): return lax.ppermute(block, both, route)  41.6 us
    all_to_all x3, blocking collectives, on_device(): lax.all_to_all(sent.reshape(XS * 2 * PAIR * ROWS, width), 'xy', 0, 0, axi...  32 us
    ppermute x6, waiting for transfers between devices, send(): return lax.ppermute(block, both, route)  19.8 us
    pallas_call x6, Pallas kernels, call(): pl.pallas_call(kernel, out_shape=outs, in_specs=[vmem] * len(arrays), out...  6.52 us
    pallas_call x1, Pallas kernels, load(): pl.pallas_call(load_kernel, out_shape=pltpu.VMEM((4,) + own[0].shape, BF)...  2.93 us
    ppermute x1, waiting for transfers between devices, on_device(): v_other = lax.ppermute(v_sent, 'xy', [(i, i ^ 1) for i in range(16)])  2.6 us
  transfers between devices with their start and end apart: 8, of which 6 were waited for; matrix products, arithmetic and copies ran while one was open for 0% of the time, Pallas kernels for 3%

profile of v5, /device:TPU:57, one launch (start us, length us, event | category | flops | bytes accessed | tf_op | source)
XLA Modules:
  0.0 116.2 jit_solution(3872863750569852411)
XLA Ops:
  0.6 0.9 shard_map.77
  1.5 2.2 %all-gather = bf16[288,256]{1,0:T(8,128)(2,1)S(1)} all-gather(bf16[144,256]{1,0:T(8,128)(2,1)S(1)} %shard_map.77), channel_id=2, replica_groups={{0,1},{2,3},{4,5},{6,7},{8,9},{10,11},{12,13},{14,15},{16,17},{18,19},{..., dimensions={0}, use_global_device_ids=true | all-gather | bytes 221184 | tf_op jit(solution)/shard_map/all_gather | solution.py:252
  3.8 2.3 %collective-permute-start.1 = (bf16[16,256,256]{2,1,0:T(8,128)(2,1)}, bf16[16,256,256]{2,1,0:T(8,128)(2,1)S(1)}, u32[]{:S(2)}, u32[]{:S(2)}) collective-permute-start(bf16[16,256,256]{2,1,0:T(8,128)(2,1)} %bitcast.29), channel_id=1, source_target_pairs={{0,1},{1,0},{2,3},{3,2},{4,5},{5,4},{6,7},{7,6},{8,9},{9,8},{10,11... | collective-permute-start | bytes 6291464 | tf_op jit(solution)/shard_map/ppermute | solution.py:256
  6.0 2.1 %collective-permute-start.2 = (bf16[16,256,256]{2,1,0:T(8,128)(2,1)}, bf16[16,256,256]{2,1,0:T(8,128)(2,1)}, u32[]{:S(2)}, u32[]{:S(2)}) collective-permute-start(bf16[16,256,256]{2,1,0:T(8,128)(2,1)} %bitcast.31), channel_id=1, source_target_pairs={{0,1},{1,0},{2,3},{3,2},{4,5},{5,4},{6,7},{7,6},{8,9},{9,8},{10,11... | collective-permute-start | bytes 6291464 | tf_op jit(solution)/shard_map/ppermute | solution.py:257
  8.2 2.4 %collective-permute-start = (bf16[2,64,256]{2,1,0:T(8,128)(2,1)S(1)}, bf16[2,64,256]{2,1,0:T(8,128)(2,1)S(1)}, u32[]{:S(2)}, u32[]{:S(2)}) collective-permute-start(bf16[2,64,256]{2,1,0:T(8,128)(2,1)S(1)} %slice_select_fusion.own0_ref), channel_id=1, source_target_pairs={{0,9},{2,11},{4,13},{6,15},{9,0},{11,2},{13,4},{15,6},{16,25},{17,... | collective-permute-start | bytes 196616 | tf_op jit(solution)/shard_map/ppermute | solution.py:228
  10.6 0.0 collective-permute-done.1.u_other
  10.6 2.6 %collective-permute-done.2.v_other = bf16[16,256,256]{2,1,0:T(8,128)(2,1)} collective-permute-done((bf16[16,256,256]{2,1,0:T(8,128)(2,1)}, bf16[16,256,256]{2,1,0:T(8,128)(2,1)}, u32[]{:S(2)}, u32[]{:S(2)}) %collective-permute-start.2) | collective-permute-done | bytes 2097184 | tf_op jit(solution)/shard_map/ppermute | solution.py:257
  13.2 2.9 %shard_map.78.held_ref = bf16[4,16,256,256]{3,2,1,0:T(8,128)(2,1)S(1)} custom-call(bf16[16,256,256]{2,1,0:T(8,128)(2,1)} %bitcast.30, bf16[16,256,256]{2,1,0:T(8,128)(2,1)} %bitcast.32, bf16[16,256,256]{2,1,0:T(8,128)(2,1)S(1)} %collective-permute-done.1.u_other, bf16[16,256,256]{2,1,0:T(8,128)(2,1)} %collective-permute-done.2.v_other), custom_call_target="tpu_custom_call" | custom-call | bytes 8388608 | tf_op jit(solution)/shard_map/pallas_call | solution.py:200
  16.1 0.0 collective-permute-done.first_ref
  16.1 2.1 %shard_map.79 = bf16[4,4,64,256]{3,2,1,0:T(8,128)(2,1)S(1)} custom-call(s32[32,128]{1,0:T(8,128)S(1)} %bitcast.23, bf16[2,64,256]{2,1,0:T(8,128)(2,1)S(1)} %slice_select_fusion.own0_ref, bf16[2,64,256]{2,1,0:T(8,128)(2,1)S(1)} %collective-permute-done.first_ref, bf16[4,16,256,256]{3,2,1,0:T(8,128)(2,1)S(1)} %shard_map.78.held_ref), custom_call_target="tpu_custom_call" | custom-call | flops 536870912 | bytes 10485760 | tf_op jit(solution)/shard_map/pallas_call | solution.py:188
  18.2 10.7 %all_to_all.27 = bf16[4,256,256]{2,1,0:T(8,128)(2,1)S(1)} all-to-all(bf16[4,256,256]{2,1,0:T(8,128)(2,1)S(1)} %bitcast.22), channel_id=1, replica_groups={{0,2,4,6},{1,3,5,7},{8,10,12,14},{9,11,13,15},{16,18,20,22},{17,19,21,2..., dimensions={0} | all-to-all | bytes 1048576 | tf_op jit(solution)/shard_map/all_to_all | solution.py:270
  29.0 0.1 shard_map.80
  29.1 16.4 %collective-permute-start.3 = (bf16[2,64,256]{2,1,0:T(8,128)(2,1)S(1)}, bf16[2,64,256]{2,1,0:T(8,128)(2,1)S(1)}, u32[]{:S(2)}, u32[]{:S(2)}) collective-permute-start(bf16[2,64,256]{2,1,0:T(8,128)(2,1)S(1)} %get-tuple-element.14), channel_id=1, source_target_pairs={{0,25},{2,27},{4,29},{6,31},{9,16},{11,18},{13,20},{15,22},{16,41}... | collective-permute-start | bytes 196616 | tf_op jit(solution)/shard_map/ppermute | solution.py:228
  45.5 2.1 %collective-permute-start.4 = (bf16[2,64,256]{2,1,0:T(8,128)(2,1)S(1)}, bf16[2,64,256]{2,1,0:T(8,128)(2,1)S(1)}, u32[]{:S(2)}, u32[]{:S(2)}) collective-permute-start(bf16[2,64,256]{2,1,0:T(8,128)(2,1)S(1)} %get-tuple-element.15), channel_id=1, source_target_pairs={{0,16},{2,18},{4,20},{6,22},{9,25},{11,27},{13,29},{15,31},{16,32}... | collective-permute-start | bytes 196616 | tf_op jit(solution)/shard_map/ppermute | solution.py:228
  47.5 0.5 collective-permute-done.3.far_ref
  48.1 5.0 %collective-permute-done.4.hop_ref = bf16[2,64,256]{2,1,0:T(8,128)(2,1)S(1)} collective-permute-done((bf16[2,64,256]{2,1,0:T(8,128)(2,1)S(1)}, bf16[2,64,256]{2,1,0:T(8,128)(2,1)S(1)}, u32[]{:S(2)}, u32[]{:S(2)}) %collective-permute-start.4) | collective-permute-done | bytes 65568 | tf_op jit(solution)/shard_map/ppermute | solution.py:228
  53.0 2.1 %shard_map.81 = bf16[4,4,64,256]{3,2,1,0:T(8,128)(2,1)S(1)} custom-call(s32[32,128]{1,0:T(8,128)S(1)} %bitcast.25, bf16[2,64,256]{2,1,0:T(8,128)(2,1)S(1)} %collective-permute-done.3.far_ref, bf16[2,64,256]{2,1,0:T(8,128)(2,1)S(1)} %collective-permute-done.4.hop_ref, bf16[2,64,256]{2,1,0:T(8,128)(2,1)S(1)} %slice_select_fusion.own0_ref, ...), custom_call_target="tpu_custom_call" | custom-call | flops 536870912 | bytes 10485760 | tf_op jit(solution)/shard_map/pallas_call | solution.py:188
  55.1 10.2 %all_to_all.28 = bf16[4,256,256]{2,1,0:T(8,128)(2,1)S(1)} all-to-all(bf16[4,256,256]{2,1,0:T(8,128)(2,1)S(1)} %bitcast.21), channel_id=1, replica_groups={{0,2,4,6},{1,3,5,7},{8,10,12,14},{9,11,13,15},{16,18,20,22},{17,19,21,2..., dimensions={0} | all-to-all | bytes 1048576 | tf_op jit(solution)/shard_map/all_to_all | solution.py:270
  65.3 0.1 shard_map.82
  65.4 8.7 %collective-permute-start.5 = (bf16[2,64,256]{2,1,0:T(8,128)(2,1)S(1)}, bf16[2,64,256]{2,1,0:T(8,128)(2,1)S(1)}, u32[]{:S(2)}, u32[]{:S(2)}) collective-permute-start(bf16[2,64,256]{2,1,0:T(8,128)(2,1)S(1)} %get-tuple-element.16), channel_id=1, source_target_pairs={{0,25},{2,27},{4,29},{6,31},{9,16},{11,18},{13,20},{15,22},{16,41}... | collective-permute-start | bytes 196616 | tf_op jit(solution)/shard_map/ppermute | solution.py:228
  74.1 2.1 %collective-permute-start.6 = (bf16[2,64,256]{2,1,0:T(8,128)(2,1)S(1)}, bf16[2,64,256]{2,1,0:T(8,128)(2,1)S(1)}, u32[]{:S(2)}, u32[]{:S(2)}) collective-permute-start(bf16[2,64,256]{2,1,0:T(8,128)(2,1)S(1)} %get-tuple-element.17), channel_id=1, source_target_pairs={{0,16},{2,18},{4,20},{6,22},{9,25},{11,27},{13,29},{15,31},{16,32}... | collective-permute-start | bytes 196616 | tf_op jit(solution)/shard_map/ppermute | solution.py:228
  76.2 5.5 %collective-permute-done.5.far_ref = bf16[2,64,256]{2,1,0:T(8,128)(2,1)S(1)} collective-permute-done((bf16[2,64,256]{2,1,0:T(8,128)(2,1)S(1)}, bf16[2,64,256]{2,1,0:T(8,128)(2,1)S(1)}, u32[]{:S(2)}, u32[]{:S(2)}) %collective-permute-start.5) | collective-permute-done | bytes 65568 | tf_op jit(solution)/shard_map/ppermute | solution.py:228
  81.7 4.0 %collective-permute-done.6.hop_ref = bf16[2,64,256]{2,1,0:T(8,128)(2,1)S(1)} collective-permute-done((bf16[2,64,256]{2,1,0:T(8,128)(2,1)S(1)}, bf16[2,64,256]{2,1,0:T(8,128)(2,1)S(1)}, u32[]{:S(2)}, u32[]{:S(2)}) %collective-permute-start.6) | collective-permute-done | bytes 65568 | tf_op jit(solution)/shard_map/ppermute | solution.py:228
  85.7 2.1 %shard_map.83 = bf16[4,4,64,256]{3,2,1,0:T(8,128)(2,1)S(1)} custom-call(s32[32,128]{1,0:T(8,128)S(1)} %bitcast.27, bf16[2,64,256]{2,1,0:T(8,128)(2,1)S(1)} %collective-permute-done.5.far_ref, bf16[2,64,256]{2,1,0:T(8,128)(2,1)S(1)} %collective-permute-done.6.hop_ref, bf16[2,64,256]{2,1,0:T(8,128)(2,1)S(1)} %slice_select_fusion.own0_ref, ...), custom_call_target="tpu_custom_call" | custom-call | flops 536870912 | bytes 10485760 | tf_op jit(solution)/shard_map/pallas_call | solution.py:188
  87.8 11.0 %all_to_all.29 = bf16[4,256,256]{2,1,0:T(8,128)(2,1)S(1)} all-to-all(bf16[4,256,256]{2,1,0:T(8,128)(2,1)S(1)} %bitcast.18), channel_id=1, replica_groups={{0,2,4,6},{1,3,5,7},{8,10,12,14},{9,11,13,15},{16,18,20,22},{17,19,21,2..., dimensions={0} | all-to-all | bytes 1048576 | tf_op jit(solution)/shard_map/all_to_all | solution.py:270
  98.8 0.1 shard_map.84
  98.9 10.0 %collective-permute-start.7 = (bf16[2,64,256]{2,1,0:T(8,128)(2,1)S(1)}, bf16[2,64,256]{2,1,0:T(8,128)(2,1)S(1)}, u32[]{:S(2)}, u32[]{:S(2)}) collective-permute-start(bf16[2,64,256]{2,1,0:T(8,128)(2,1)S(1)} %get-tuple-element.19), channel_id=1, source_target_pairs={{0,16},{1,8},{2,18},{3,10},{4,20},{5,12},{6,22},{7,14},{8,1},{9,25... | collective-permute-start | bytes 196616 | tf_op jit(solution)/shard_map/ppermute | solution.py:228
  108.9 4.8 %collective-permute-done.7 = bf16[2,64,256]{2,1,0:T(8,128)(2,1)S(1)} collective-permute-done((bf16[2,64,256]{2,1,0:T(8,128)(2,1)S(1)}, bf16[2,64,256]{2,1,0:T(8,128)(2,1)S(1)}, u32[]{:S(2)}, u32[]{:S(2)}) %collective-permute-start.7) | collective-permute-done | bytes 65568 | tf_op jit(solution)/shard_map/ppermute | solution.py:228
  113.7 1.9 %all_gather.11 = bf16[2,64,256]{2,1,0:T(8,128)(2,1)S(1)} all-gather(bf16[1,64,256]{2,1,0:T(8,128)(2,1)S(1)} %constant_dynamic-slice_fusion), channel_id=1, replica_groups={{0,1},{2,3},{4,5},{6,7},{8,9},{10,11},{12,13},{14,15},{16,17},{18,19},{..., dimensions={0}, use_global_device_ids=true | all-gather | bytes 98304 | tf_op jit(solution)/shard_map/all_gather | solution.py:280
  115.6 0.6 broadcast_select_fusion
  (4 shorter events, 0.1 us)
Async XLA Ops:
  3.8 6.8 %collective-permute-start.1 = (bf16[16,256,256]{2,1,0:T(8,128)(2,1)}, bf16[16,256,256]{2,1,0:T(8,128)(2,1)S(1)}, u32[]{:S(2)}, u32[]{:S(2)}) collective-permute-start(bf16[16,256,256]{2,1,0:T(8,128)(2,1)} %bitcast.29), channel_id=1, source_target_pairs={{0,1},{1,0},{2,3},{3,2},{4,5},{5,4},{6,7},{7,6},{8,9},{9,8},{10,11... | collective-permute-start | bytes 6291464 | tf_op jit(solution)/shard_map/ppermute | solution.py:256
  6.0 7.1 %collective-permute-start.2 = (bf16[16,256,256]{2,1,0:T(8,128)(2,1)}, bf16[16,256,256]{2,1,0:T(8,128)(2,1)}, u32[]{:S(2)}, u32[]{:S(2)}) collective-permute-start(bf16[16,256,256]{2,1,0:T(8,128)(2,1)} %bitcast.31), channel_id=1, source_target_pairs={{0,1},{1,0},{2,3},{3,2},{4,5},{5,4},{6,7},{7,6},{8,9},{9,8},{10,11... | collective-permute-start | bytes 6291464 | tf_op jit(solution)/shard_map/ppermute | solution.py:257
  8.2 7.9 %collective-permute-start = (bf16[2,64,256]{2,1,0:T(8,128)(2,1)S(1)}, bf16[2,64,256]{2,1,0:T(8,128)(2,1)S(1)}, u32[]{:S(2)}, u32[]{:S(2)}) collective-permute-start(bf16[2,64,256]{2,1,0:T(8,128)(2,1)S(1)} %slice_select_fusion.own0_ref), channel_id=1, source_target_pairs={{0,9},{2,11},{4,13},{6,15},{9,0},{11,2},{13,4},{15,6},{16,25},{17,... | collective-permute-start | bytes 196616 | tf_op jit(solution)/shard_map/ppermute | solution.py:228
  29.1 19.0 %collective-permute-start.3 = (bf16[2,64,256]{2,1,0:T(8,128)(2,1)S(1)}, bf16[2,64,256]{2,1,0:T(8,128)(2,1)S(1)}, u32[]{:S(2)}, u32[]{:S(2)}) collective-permute-start(bf16[2,64,256]{2,1,0:T(8,128)(2,1)S(1)} %get-tuple-element.14), channel_id=1, source_target_pairs={{0,25},{2,27},{4,29},{6,31},{9,16},{11,18},{13,20},{15,22},{16,41}... | collective-permute-start | bytes 196616 | tf_op jit(solution)/shard_map/ppermute | solution.py:228
  45.5 7.6 %collective-permute-start.4 = (bf16[2,64,256]{2,1,0:T(8,128)(2,1)S(1)}, bf16[2,64,256]{2,1,0:T(8,128)(2,1)S(1)}, u32[]{:S(2)}, u32[]{:S(2)}) collective-permute-start(bf16[2,64,256]{2,1,0:T(8,128)(2,1)S(1)} %get-tuple-element.15), channel_id=1, source_target_pairs={{0,16},{2,18},{4,20},{6,22},{9,25},{11,27},{13,29},{15,31},{16,32}... | collective-permute-start | bytes 196616 | tf_op jit(solution)/shard_map/ppermute | solution.py:228
  65.4 16.3 %collective-permute-start.5 = (bf16[2,64,256]{2,1,0:T(8,128)(2,1)S(1)}, bf16[2,64,256]{2,1,0:T(8,128)(2,1)S(1)}, u32[]{:S(2)}, u32[]{:S(2)}) collective-permute-start(bf16[2,64,256]{2,1,0:T(8,128)(2,1)S(1)} %get-tuple-element.16), channel_id=1, source_target_pairs={{0,25},{2,27},{4,29},{6,31},{9,16},{11,18},{13,20},{15,22},{16,41}... | collective-permute-start | bytes 196616 | tf_op jit(solution)/shard_map/ppermute | solution.py:228
  74.1 11.6 %collective-permute-start.6 = (bf16[2,64,256]{2,1,0:T(8,128)(2,1)S(1)}, bf16[2,64,256]{2,1,0:T(8,128)(2,1)S(1)}, u32[]{:S(2)}, u32[]{:S(2)}) collective-permute-start(bf16[2,64,256]{2,1,0:T(8,128)(2,1)S(1)} %get-tuple-element.17), channel_id=1, source_target_pairs={{0,16},{2,18},{4,20},{6,22},{9,25},{11,27},{13,29},{15,31},{16,32}... | collective-permute-start | bytes 196616 | tf_op jit(solution)/shard_map/ppermute | solution.py:228
  98.9 14.8 %collective-permute-start.7 = (bf16[2,64,256]{2,1,0:T(8,128)(2,1)S(1)}, bf16[2,64,256]{2,1,0:T(8,128)(2,1)S(1)}, u32[]{:S(2)}, u32[]{:S(2)}) collective-permute-start(bf16[2,64,256]{2,1,0:T(8,128)(2,1)S(1)} %get-tuple-element.19), channel_id=1, source_target_pairs={{0,16},{1,8},{2,18},{3,10},{4,20},{5,12},{6,22},{7,14},{8,1},{9,25... | collective-permute-start | bytes 196616 | tf_op jit(solution)/shard_map/ppermute | solution.py:228

commit v6 on v5

--- a/solution.py
+++ b/solution.py
@@ -170,8 +170,8 @@
     return jnp.sum(picked, axis=1, keepdims=True)
 
 
-def pack_kernel(layer_ref, source_ref, rank_ref, up_ref, down_ref, packed_ref):
-    layer = layer_ref[0]
+def pack_kernel(source_ref, rank_ref, up_ref, down_ref, packed_ref):
+    layer = lax.axis_index("gz")
     width = packed_ref.shape[1]
     sources = jnp.broadcast_to(column(source_ref[...], HALF), (HALF, width))
     zero = jnp.zeros((HALF, width), BF)
@@ -209,7 +209,6 @@
 
 
 def on_device(layers, up_source, down_source, source_layer, u_factor, v_factor, block_rank):
-    layer = lax.axis_index("gz")
     place = lax.axis_index("xy")
     core = place % 2
     up_here = (place + place // 8) % 2 == 0
@@ -246,9 +245,9 @@
     packed = pl.pallas_call(
         pack_kernel,
         out_shape=pltpu.VMEM((2 * ROWS + 16, width), BF),
-        in_specs=[pl.BlockSpec(memory_space=pltpu.SMEM)] + [vmem] * 4,
+        in_specs=[vmem] * 4,
         out_specs=vmem,
-    )(layer.astype(jnp.int32)[None], source_layer[None], block_rank[0], up_source[0], down_source[0])
+    )(source_layer[None], block_rank[0], up_source[0], down_source[0])
     chip = lax.all_gather(packed, "xy", axis=0, axis_index_groups=pairs)
     u_own = u_factor[0, 0].reshape(16, 2 * max_rank, width)
     v_own = v_factor[0, 0].reshape(16, 2 * max_rank, width)

time: 117 us -> 117 us (level)
  no operation moved by 1% of the time
where the time goes in v6:
time: 117 us; the launch traced here: 116 us
  starting transfers between devices  45.9 us (39%)
  blocking collectives  36.1 us (31%)
  waiting for transfers between devices  22.4 us (19%)
  Pallas kernels  10.3 us (9%)
    ppermute x6, starting transfers between devices, send(): return lax.ppermute(block, both, route)  41.6 us
    all_to_all x3, blocking collectives, on_device(): lax.all_to_all(sent.reshape(XS * 2 * PAIR * ROWS, width), 'xy', 0, 0, axi...  32 us
    ppermute x6, waiting for transfers between devices, send(): return lax.ppermute(block, both, route)  19.8 us
    pallas_call x6, Pallas kernels, call(): pl.pallas_call(kernel, out_shape=outs, in_specs=[vmem] * len(arrays), out...  6.52 us
    pallas_call x1, Pallas kernels, load(): pl.pallas_call(load_kernel, out_shape=pltpu.VMEM((4,) + own[0].shape, BF)...  2.93 us
    ppermute x1, waiting for transfers between devices, on_device(): v_other = lax.ppermute(v_sent, 'xy', [(i, i ^ 1) for i in range(16)])  2.6 us
  transfers between devices with their start and end apart: 8, of which 6 were waited for; matrix products, arithmetic and copies ran while one was open for 0% of the time, Pallas kernels for 3%

profile of v6, /device:TPU:57, one launch (start us, length us, event | category | flops | bytes accessed | tf_op | source)
XLA Modules:
  0.0 116.2 jit_solution(905205726303184246)
XLA Ops:
  0.6 0.9 shard_map.77
  1.5 2.2 %all-gather = bf16[288,256]{1,0:T(8,128)(2,1)S(1)} all-gather(bf16[144,256]{1,0:T(8,128)(2,1)S(1)} %shard_map.77), channel_id=2, replica_groups={{0,1},{2,3},{4,5},{6,7},{8,9},{10,11},{12,13},{14,15},{16,17},{18,19},{..., dimensions={0}, use_global_device_ids=true | all-gather | bytes 221184 | tf_op jit(solution)/shard_map/all_gather | solution.py:251
  3.8 2.3 %collective-permute-start.1 = (bf16[16,256,256]{2,1,0:T(8,128)(2,1)}, bf16[16,256,256]{2,1,0:T(8,128)(2,1)S(1)}, u32[]{:S(2)}, u32[]{:S(2)}) collective-permute-start(bf16[16,256,256]{2,1,0:T(8,128)(2,1)} %bitcast.28), channel_id=1, source_target_pairs={{0,1},{1,0},{2,3},{3,2},{4,5},{5,4},{6,7},{7,6},{8,9},{9,8},{10,11... | collective-permute-start | bytes 6291464 | tf_op jit(solution)/shard_map/ppermute | solution.py:255
  6.0 2.1 %collective-permute-start.2 = (bf16[16,256,256]{2,1,0:T(8,128)(2,1)}, bf16[16,256,256]{2,1,0:T(8,128)(2,1)}, u32[]{:S(2)}, u32[]{:S(2)}) collective-permute-start(bf16[16,256,256]{2,1,0:T(8,128)(2,1)} %bitcast.30), channel_id=1, source_target_pairs={{0,1},{1,0},{2,3},{3,2},{4,5},{5,4},{6,7},{7,6},{8,9},{9,8},{10,11... | collective-permute-start | bytes 6291464 | tf_op jit(solution)/shard_map/ppermute | solution.py:256
  8.2 2.4 %collective-permute-start = (bf16[2,64,256]{2,1,0:T(8,128)(2,1)S(1)}, bf16[2,64,256]{2,1,0:T(8,128)(2,1)S(1)}, u32[]{:S(2)}, u32[]{:S(2)}) collective-permute-start(bf16[2,64,256]{2,1,0:T(8,128)(2,1)S(1)} %slice_select_fusion.own0_ref), channel_id=1, source_target_pairs={{0,9},{2,11},{4,13},{6,15},{9,0},{11,2},{13,4},{15,6},{16,25},{17,... | collective-permute-start | bytes 196616 | tf_op jit(solution)/shard_map/ppermute | solution.py:227
  10.6 0.0 collective-permute-done.1.u_other
  10.6 2.6 %collective-permute-done.2.v_other = bf16[16,256,256]{2,1,0:T(8,128)(2,1)} collective-permute-done((bf16[16,256,256]{2,1,0:T(8,128)(2,1)}, bf16[16,256,256]{2,1,0:T(8,128)(2,1)}, u32[]{:S(2)}, u32[]{:S(2)}) %collective-permute-start.2) | collective-permute-done | bytes 2097184 | tf_op jit(solution)/shard_map/ppermute | solution.py:256
  13.2 2.9 %shard_map.78.held_ref = bf16[4,16,256,256]{3,2,1,0:T(8,128)(2,1)S(1)} custom-call(bf16[16,256,256]{2,1,0:T(8,128)(2,1)} %bitcast.29, bf16[16,256,256]{2,1,0:T(8,128)(2,1)} %bitcast.31, bf16[16,256,256]{2,1,0:T(8,128)(2,1)S(1)} %collective-permute-done.1.u_other, bf16[16,256,256]{2,1,0:T(8,128)(2,1)} %collective-permute-done.2.v_other), custom_call_target="tpu_custom_call" | custom-call | bytes 8388608 | tf_op jit(solution)/shard_map/pallas_call | solution.py:200
  16.1 0.0 collective-permute-done.first_ref
  16.1 2.1 %shard_map.79 = bf16[4,4,64,256]{3,2,1,0:T(8,128)(2,1)S(1)} custom-call(s32[32,128]{1,0:T(8,128)S(1)} %bitcast.22, bf16[2,64,256]{2,1,0:T(8,128)(2,1)S(1)} %slice_select_fusion.own0_ref, bf16[2,64,256]{2,1,0:T(8,128)(2,1)S(1)} %collective-permute-done.first_ref, bf16[4,16,256,256]{3,2,1,0:T(8,128)(2,1)S(1)} %shard_map.78.held_ref), custom_call_target="tpu_custom_call" | custom-call | flops 536870912 | bytes 10485760 | tf_op jit(solution)/shard_map/pallas_call | solution.py:188
  18.2 10.8 %all_to_all.27 = bf16[4,256,256]{2,1,0:T(8,128)(2,1)S(1)} all-to-all(bf16[4,256,256]{2,1,0:T(8,128)(2,1)S(1)} %bitcast.21), channel_id=1, replica_groups={{0,2,4,6},{1,3,5,7},{8,10,12,14},{9,11,13,15},{16,18,20,22},{17,19,21,2..., dimensions={0} | all-to-all | bytes 1048576 | tf_op jit(solution)/shard_map/all_to_all | solution.py:269
  29.0 0.1 shard_map.80
  29.1 16.4 %collective-permute-start.3 = (bf16[2,64,256]{2,1,0:T(8,128)(2,1)S(1)}, bf16[2,64,256]{2,1,0:T(8,128)(2,1)S(1)}, u32[]{:S(2)}, u32[]{:S(2)}) collective-permute-start(bf16[2,64,256]{2,1,0:T(8,128)(2,1)S(1)} %get-tuple-element.14), channel_id=1, source_target_pairs={{0,25},{2,27},{4,29},{6,31},{9,16},{11,18},{13,20},{15,22},{16,41}... | collective-permute-start | bytes 196616 | tf_op jit(solution)/shard_map/ppermute | solution.py:227
  45.5 2.1 %collective-permute-start.4 = (bf16[2,64,256]{2,1,0:T(8,128)(2,1)S(1)}, bf16[2,64,256]{2,1,0:T(8,128)(2,1)S(1)}, u32[]{:S(2)}, u32[]{:S(2)}) collective-permute-start(bf16[2,64,256]{2,1,0:T(8,128)(2,1)S(1)} %get-tuple-element.15), channel_id=1, source_target_pairs={{0,16},{2,18},{4,20},{6,22},{9,25},{11,27},{13,29},{15,31},{16,32}... | collective-permute-start | bytes 196616 | tf_op jit(solution)/shard_map/ppermute | solution.py:227
  47.5 0.5 collective-permute-done.3.far_ref
  48.1 5.0 %collective-permute-done.4.hop_ref = bf16[2,64,256]{2,1,0:T(8,128)(2,1)S(1)} collective-permute-done((bf16[2,64,256]{2,1,0:T(8,128)(2,1)S(1)}, bf16[2,64,256]{2,1,0:T(8,128)(2,1)S(1)}, u32[]{:S(2)}, u32[]{:S(2)}) %collective-permute-start.4) | collective-permute-done | bytes 65568 | tf_op jit(solution)/shard_map/ppermute | solution.py:227
  53.0 2.1 %shard_map.81 = bf16[4,4,64,256]{3,2,1,0:T(8,128)(2,1)S(1)} custom-call(s32[32,128]{1,0:T(8,128)S(1)} %bitcast.24, bf16[2,64,256]{2,1,0:T(8,128)(2,1)S(1)} %collective-permute-done.3.far_ref, bf16[2,64,256]{2,1,0:T(8,128)(2,1)S(1)} %collective-permute-done.4.hop_ref, bf16[2,64,256]{2,1,0:T(8,128)(2,1)S(1)} %slice_select_fusion.own0_ref, ...), custom_call_target="tpu_custom_call" | custom-call | flops 536870912 | bytes 10485760 | tf_op jit(solution)/shard_map/pallas_call | solution.py:188
  55.1 10.2 %all_to_all.28 = bf16[4,256,256]{2,1,0:T(8,128)(2,1)S(1)} all-to-all(bf16[4,256,256]{2,1,0:T(8,128)(2,1)S(1)} %bitcast.20), channel_id=1, replica_groups={{0,2,4,6},{1,3,5,7},{8,10,12,14},{9,11,13,15},{16,18,20,22},{17,19,21,2..., dimensions={0} | all-to-all | bytes 1048576 | tf_op jit(solution)/shard_map/all_to_all | solution.py:269
  65.3 0.1 shard_map.82
  65.4 8.7 %collective-permute-start.5 = (bf16[2,64,256]{2,1,0:T(8,128)(2,1)S(1)}, bf16[2,64,256]{2,1,0:T(8,128)(2,1)S(1)}, u32[]{:S(2)}, u32[]{:S(2)}) collective-permute-start(bf16[2,64,256]{2,1,0:T(8,128)(2,1)S(1)} %get-tuple-element.16), channel_id=1, source_target_pairs={{0,25},{2,27},{4,29},{6,31},{9,16},{11,18},{13,20},{15,22},{16,41}... | collective-permute-start | bytes 196616 | tf_op jit(solution)/shard_map/ppermute | solution.py:227
  74.1 2.1 %collective-permute-start.6 = (bf16[2,64,256]{2,1,0:T(8,128)(2,1)S(1)}, bf16[2,64,256]{2,1,0:T(8,128)(2,1)S(1)}, u32[]{:S(2)}, u32[]{:S(2)}) collective-permute-start(bf16[2,64,256]{2,1,0:T(8,128)(2,1)S(1)} %get-tuple-element.17), channel_id=1, source_target_pairs={{0,16},{2,18},{4,20},{6,22},{9,25},{11,27},{13,29},{15,31},{16,32}... | collective-permute-start | bytes 196616 | tf_op jit(solution)/shard_map/ppermute | solution.py:227
  76.2 5.5 %collective-permute-done.5.far_ref = bf16[2,64,256]{2,1,0:T(8,128)(2,1)S(1)} collective-permute-done((bf16[2,64,256]{2,1,0:T(8,128)(2,1)S(1)}, bf16[2,64,256]{2,1,0:T(8,128)(2,1)S(1)}, u32[]{:S(2)}, u32[]{:S(2)}) %collective-permute-start.5) | collective-permute-done | bytes 65568 | tf_op jit(solution)/shard_map/ppermute | solution.py:227
  81.7 4.0 %collective-permute-done.6.hop_ref = bf16[2,64,256]{2,1,0:T(8,128)(2,1)S(1)} collective-permute-done((bf16[2,64,256]{2,1,0:T(8,128)(2,1)S(1)}, bf16[2,64,256]{2,1,0:T(8,128)(2,1)S(1)}, u32[]{:S(2)}, u32[]{:S(2)}) %collective-permute-start.6) | collective-permute-done | bytes 65568 | tf_op jit(solution)/shard_map/ppermute | solution.py:227
  85.7 2.1 %shard_map.83 = bf16[4,4,64,256]{3,2,1,0:T(8,128)(2,1)S(1)} custom-call(s32[32,128]{1,0:T(8,128)S(1)} %bitcast.26, bf16[2,64,256]{2,1,0:T(8,128)(2,1)S(1)} %collective-permute-done.5.far_ref, bf16[2,64,256]{2,1,0:T(8,128)(2,1)S(1)} %collective-permute-done.6.hop_ref, bf16[2,64,256]{2,1,0:T(8,128)(2,1)S(1)} %slice_select_fusion.own0_ref, ...), custom_call_target="tpu_custom_call" | custom-call | flops 536870912 | bytes 10485760 | tf_op jit(solution)/shard_map/pallas_call | solution.py:188
  87.8 11.0 %all_to_all.29 = bf16[4,256,256]{2,1,0:T(8,128)(2,1)S(1)} all-to-all(bf16[4,256,256]{2,1,0:T(8,128)(2,1)S(1)} %bitcast.17), channel_id=1, replica_groups={{0,2,4,6},{1,3,5,7},{8,10,12,14},{9,11,13,15},{16,18,20,22},{17,19,21,2..., dimensions={0} | all-to-all | bytes 1048576 | tf_op jit(solution)/shard_map/all_to_all | solution.py:269
  98.8 0.1 shard_map.84
  98.9 10.0 %collective-permute-start.7 = (bf16[2,64,256]{2,1,0:T(8,128)(2,1)S(1)}, bf16[2,64,256]{2,1,0:T(8,128)(2,1)S(1)}, u32[]{:S(2)}, u32[]{:S(2)}) collective-permute-start(bf16[2,64,256]{2,1,0:T(8,128)(2,1)S(1)} %get-tuple-element.19), channel_id=1, source_target_pairs={{0,16},{1,8},{2,18},{3,10},{4,20},{5,12},{6,22},{7,14},{8,1},{9,25... | collective-permute-start | bytes 196616 | tf_op jit(solution)/shard_map/ppermute | solution.py:227
  108.9 4.8 %collective-permute-done.7 = bf16[2,64,256]{2,1,0:T(8,128)(2,1)S(1)} collective-permute-done((bf16[2,64,256]{2,1,0:T(8,128)(2,1)S(1)}, bf16[2,64,256]{2,1,0:T(8,128)(2,1)S(1)}, u32[]{:S(2)}, u32[]{:S(2)}) %collective-permute-start.7) | collective-permute-done | bytes 65568 | tf_op jit(solution)/shard_map/ppermute | solution.py:227
  113.7 1.9 %all_gather.11 = bf16[2,64,256]{2,1,0:T(8,128)(2,1)S(1)} all-gather(bf16[1,64,256]{2,1,0:T(8,128)(2,1)S(1)} %constant_dynamic-slice_fusion), channel_id=1, replica_groups={{0,1},{2,3},{4,5},{6,7},{8,9},{10,11},{12,13},{14,15},{16,17},{18,19},{..., dimensions={0}, use_global_device_ids=true | all-gather | bytes 98304 | tf_op jit(solution)/shard_map/all_gather | solution.py:279
  115.5 0.6 broadcast_select_fusion
  (4 shorter events, 0.1 us)
Async XLA Ops:
  3.8 6.8 %collective-permute-start.1 = (bf16[16,256,256]{2,1,0:T(8,128)(2,1)}, bf16[16,256,256]{2,1,0:T(8,128)(2,1)S(1)}, u32[]{:S(2)}, u32[]{:S(2)}) collective-permute-start(bf16[16,256,256]{2,1,0:T(8,128)(2,1)} %bitcast.28), channel_id=1, source_target_pairs={{0,1},{1,0},{2,3},{3,2},{4,5},{5,4},{6,7},{7,6},{8,9},{9,8},{10,11... | collective-permute-start | bytes 6291464 | tf_op jit(solution)/shard_map/ppermute | solution.py:255
  6.0 7.1 %collective-permute-start.2 = (bf16[16,256,256]{2,1,0:T(8,128)(2,1)}, bf16[16,256,256]{2,1,0:T(8,128)(2,1)}, u32[]{:S(2)}, u32[]{:S(2)}) collective-permute-start(bf16[16,256,256]{2,1,0:T(8,128)(2,1)} %bitcast.30), channel_id=1, source_target_pairs={{0,1},{1,0},{2,3},{3,2},{4,5},{5,4},{6,7},{7,6},{8,9},{9,8},{10,11... | collective-permute-start | bytes 6291464 | tf_op jit(solution)/shard_map/ppermute | solution.py:256
  8.2 7.9 %collective-permute-start = (bf16[2,64,256]{2,1,0:T(8,128)(2,1)S(1)}, bf16[2,64,256]{2,1,0:T(8,128)(2,1)S(1)}, u32[]{:S(2)}, u32[]{:S(2)}) collective-permute-start(bf16[2,64,256]{2,1,0:T(8,128)(2,1)S(1)} %slice_select_fusion.own0_ref), channel_id=1, source_target_pairs={{0,9},{2,11},{4,13},{6,15},{9,0},{11,2},{13,4},{15,6},{16,25},{17,... | collective-permute-start | bytes 196616 | tf_op jit(solution)/shard_map/ppermute | solution.py:227
  29.1 19.0 %collective-permute-start.3 = (bf16[2,64,256]{2,1,0:T(8,128)(2,1)S(1)}, bf16[2,64,256]{2,1,0:T(8,128)(2,1)S(1)}, u32[]{:S(2)}, u32[]{:S(2)}) collective-permute-start(bf16[2,64,256]{2,1,0:T(8,128)(2,1)S(1)} %get-tuple-element.14), channel_id=1, source_target_pairs={{0,25},{2,27},{4,29},{6,31},{9,16},{11,18},{13,20},{15,22},{16,41}... | collective-permute-start | bytes 196616 | tf_op jit(solution)/shard_map/ppermute | solution.py:227
  45.5 7.6 %collective-permute-start.4 = (bf16[2,64,256]{2,1,0:T(8,128)(2,1)S(1)}, bf16[2,64,256]{2,1,0:T(8,128)(2,1)S(1)}, u32[]{:S(2)}, u32[]{:S(2)}) collective-permute-start(bf16[2,64,256]{2,1,0:T(8,128)(2,1)S(1)} %get-tuple-element.15), channel_id=1, source_target_pairs={{0,16},{2,18},{4,20},{6,22},{9,25},{11,27},{13,29},{15,31},{16,32}... | collective-permute-start | bytes 196616 | tf_op jit(solution)/shard_map/ppermute | solution.py:227
  65.4 16.3 %collective-permute-start.5 = (bf16[2,64,256]{2,1,0:T(8,128)(2,1)S(1)}, bf16[2,64,256]{2,1,0:T(8,128)(2,1)S(1)}, u32[]{:S(2)}, u32[]{:S(2)}) collective-permute-start(bf16[2,64,256]{2,1,0:T(8,128)(2,1)S(1)} %get-tuple-element.16), channel_id=1, source_target_pairs={{0,25},{2,27},{4,29},{6,31},{9,16},{11,18},{13,20},{15,22},{16,41}... | collective-permute-start | bytes 196616 | tf_op jit(solution)/shard_map/ppermute | solution.py:227
  74.1 11.6 %collective-permute-start.6 = (bf16[2,64,256]{2,1,0:T(8,128)(2,1)S(1)}, bf16[2,64,256]{2,1,0:T(8,128)(2,1)S(1)}, u32[]{:S(2)}, u32[]{:S(2)}) collective-permute-start(bf16[2,64,256]{2,1,0:T(8,128)(2,1)S(1)} %get-tuple-element.17), channel_id=1, source_target_pairs={{0,16},{2,18},{4,20},{6,22},{9,25},{11,27},{13,29},{15,31},{16,32}... | collective-permute-start | bytes 196616 | tf_op jit(solution)/shard_map/ppermute | solution.py:227
  98.9 14.8 %collective-permute-start.7 = (bf16[2,64,256]{2,1,0:T(8,128)(2,1)S(1)}, bf16[2,64,256]{2,1,0:T(8,128)(2,1)S(1)}, u32[]{:S(2)}, u32[]{:S(2)}) collective-permute-start(bf16[2,64,256]{2,1,0:T(8,128)(2,1)S(1)} %get-tuple-element.19), channel_id=1, source_target_pairs={{0,16},{1,8},{2,18},{3,10},{4,20},{5,12},{6,22},{7,14},{8,1},{9,25... | collective-permute-start | bytes 196616 | tf_op jit(solution)/shard_map/ppermute | solution.py:227
